TPU v7x, 32 devices: a whole 2x2x4 slice. The times are simulated.
32 devices in a mesh: vocab: 16 (over z, x, core), grp: 2 (over y).
Axes of the slice: x: 2, y: 2, z: 4, core: 2. Of those that a mesh axis runs over, the one named last changes fastest.
Arguments:
- hidden: bfloat16 [512, 4096], P('grp'), may hold values from -240 to 240
- head_weight: bfloat16 [4096, 32768], P('grp', 'vocab'), may hold values from -0.25 to 0.25
- cluster_weight: bfloat16 [4096, 3], replicated, may hold values from -0.5 to 0.5
- proj_one: bfloat16 [4096, 1024], P('vocab'), may hold values from -0.09375 to 0.09375
- proj_two: bfloat16 [4096, 256], P('vocab'), may hold values from -0.09375 to 0.09375
- proj_three: bfloat16 [4096, 64], P('vocab'), may hold values from -0.09375 to 0.09375
- tail_one: bfloat16 [1024, 65536], P('grp', 'vocab'), may hold values from -0.5 to 0.5
- tail_two: bfloat16 [256, 65536], P('grp', 'vocab'), may hold values from -1 to 1
- tail_three: bfloat16 [64, 65536], P('grp', 'vocab'), may hold values from -2 to 2
- targets: int32 [512], P('grp'), may hold values from 0 to 229375, as said below
- flags: int32 [512, 3], P('grp'), may hold values from 0 to 1, as said below
Outputs:
- target_logprob: float32 [512], P('grp')
- tail_entropy: float32 [512, 3], P('grp')
Inputs may be any that keep to these rules, and one draw needn't show every extreme that they name: `targets`: a target at or beyond 32768 lies in tail (t - 32768) // 65536. flags[b, c] is 1 whenever the target of sequence b lies in tail c.
All inputs are finite; a program needn't handle non-finite values.
Results may differ from a plain program's by a relative error of at most 0.0092.
Values may be sent and summed in bfloat16 or wider, within the bound.
A program may use at most 128 MiB of HBM per device.

v0:
```python
import jax
import jax.numpy as jnp
from jax import lax
from jax.sharding import PartitionSpec as P

V_HEAD = 32768
TAIL = 65536


def shards(
    hidden,
    head_weight,
    cluster_weight,
    proj_one,
    proj_two,
    proj_three,
    tail_one,
    tail_two,
    tail_three,
    targets,
    flags,
):
    rows = hidden.shape[0]
    head_cols = head_weight.shape[1]
    vocab_index = lax.axis_index("vocab")
    every_row = lax.all_to_all(hidden, "grp", split_axis=1, concat_axis=0, tiled=True)
    partial_logits = jnp.dot(every_row, head_weight, preferred_element_type=jnp.float32)
    head_logits = lax.psum_scatter(partial_logits, "grp", scatter_dimension=0, tiled=True)
    cluster_score_logits = jnp.dot(hidden, cluster_weight, preferred_element_type=jnp.float32)
    width_voc = proj_one.shape[0]
    features = lax.dynamic_slice_in_dim(hidden, vocab_index * width_voc, width_voc, 1)
    partial_proj = tuple(
        (
            jnp.dot(features, weight, preferred_element_type=jnp.float32)
            for weight in (proj_one, proj_two, proj_three)
        )
    )
    summed = lax.psum(partial_proj, "vocab")
    projected = [value.astype(jnp.bfloat16) for value in summed]
    full_tails = (
        lax.all_gather(tail_one, "grp", axis=0, tiled=True),
        lax.all_gather(tail_two, "grp", axis=0, tiled=True),
        lax.all_gather(tail_three, "grp", axis=0, tiled=True),
    )
    tail_cluster_logits = jnp.stack(
        [
            jnp.dot(projected[index], full_tails[index], preferred_element_type=jnp.float32)
            for index in range(3)
        ],
        axis=0,
    )
    tail_cols = tail_cluster_logits.shape[2]
    head_ids = vocab_index * head_cols + jnp.arange(head_cols, dtype=jnp.int32)
    head_pick = jnp.sum(jnp.where(head_ids[None, :] == targets[:, None], head_logits, 0.0), axis=1)
    relative = targets - V_HEAD
    cluster = relative // TAIL
    word = relative - cluster * TAIL
    tail_ids = vocab_index * tail_cols + jnp.arange(tail_cols, dtype=jnp.int32)
    same_word = tail_ids[None, :] == word[:, None]
    tail_pick = jnp.zeros((rows,), jnp.float32)
    for index in range(3):
        hit = jnp.logical_and(same_word, (cluster == index)[:, None])
        tail_pick = tail_pick + jnp.sum(jnp.where(hit, tail_cluster_logits[index], 0.0), axis=1)
    picked = head_pick + tail_pick
    local_head_max = jnp.max(head_logits, axis=1)
    local_tail_max = jnp.transpose(jnp.max(tail_cluster_logits, axis=2))
    head_max, tail_max = lax.pmax((local_head_max, local_tail_max), "vocab")
    head_sum = jnp.sum(jnp.exp(head_logits - head_max[:, None]), axis=1)
    expo = jnp.exp(tail_cluster_logits - jnp.transpose(tail_max)[:, :, None])
    tail_sum = jnp.transpose(jnp.sum(expo, axis=2))
    tail_weighted = jnp.transpose(jnp.sum(expo * tail_cluster_logits, axis=2))
    head_sum, tail_sum, tail_weighted, picked = lax.psum(
        (head_sum, tail_sum, tail_weighted, picked), "vocab"
    )
    top = jnp.maximum(head_max, jnp.max(cluster_score_logits, axis=1))
    total = head_sum * jnp.exp(head_max - top) + jnp.sum(
        jnp.exp(cluster_score_logits - top[:, None]), axis=1
    )
    head_lse = top + jnp.log(total)
    tail_lse = tail_max + jnp.log(tail_sum)
    tail_mean = tail_weighted / tail_sum
    tail_entropy = flags.astype(jnp.float32) * (tail_lse - tail_mean)
    which = cluster[:, None] == jnp.arange(3, dtype=jnp.int32)[None, :]
    cluster_term = jnp.sum(jnp.where(which, cluster_score_logits - tail_lse, 0.0), axis=1)
    target_logprob = jnp.where(targets < V_HEAD, picked, picked + cluster_term) - head_lse
    return (target_logprob, tail_entropy)


def solution(mesh):
    return jax.shard_map(
        shards,
        mesh=mesh,
        in_specs=(
            P("grp", None),
            P("grp", "vocab"),
            P(),
            P("vocab", None),
            P("vocab", None),
            P("vocab", None),
            P("grp", "vocab"),
            P("grp", "vocab"),
            P("grp", "vocab"),
            P("grp"),
            P("grp", None),
        ),
        out_specs=(P("grp"), P("grp", None)),
        check_vma=False,
    )
```

profile of v0, /device:TPU:1, one launch (start us, length us, event | category | flops | bytes accessed | tf_op | source)
XLA Modules:
  0.0 333.2 jit_solution(7610174767980583788)
XLA Ops:
  7.2 0.0 copy-start
  7.2 0.0 copy-start.4
  7.2 0.0 all-gather.3.cloned.1.call-start
  7.2 0.7 all-gather.3.cloned.1.call-update
  7.9 0.9 copy-done.4
  8.8 2.5 copy.13
  11.3 4.9 %all-to-all-start = ((bf16[256,2,2048]{0,2,1:T(8,128)(2,1)}), bf16[256,2,2048]{0,2,1:T(8,128)(2,1)}, u32[]{:S(2)}, u32[]{:S(2)}) async-start(bf16[256,2,2048]{0,2,1:T(8,128)(2,1)} %bitcast.29), calls=%async_computation | async-start | bytes 4194304 | tf_op jit(solution)/shard_map/all_to_all | solution.py:26
  16.2 0.0 all-gather.5.cloned.1.call-start
  16.2 0.7 all-gather.5.cloned.1.call-update
  16.9 0.0 reduce-scatter.2.cloned.1.call-start
  17.0 39.6 %all-to-all-done = bf16[256,2,2048]{0,2,1:T(8,128)(2,1)} async-done(((bf16[256,2,2048]{0,2,1:T(8,128)(2,1)}), bf16[256,2,2048]{0,2,1:T(8,128)(2,1)}, u32[]{:S(2)}, u32[]{:S(2)}) %all-to-all-start) | async-done | bytes 2097184 | tf_op jit(solution)/shard_map/all_to_all | solution.py:26
  56.6 4.0 %copy.14 = bf16[2,256,2048]{2,1,0:T(8,128)(2,1)} copy(bf16[2,256,2048]{1,2,0:T(8,128)(2,1)} %bitcast.1) | data formatting | bytes 4194304 | tf_op jit(solution)/shard_map/all_to_all | solution.py:26
  60.6 10.5 %fusion.19 = f32[512,2048]{1,0:T(8,128)} fusion(bf16[512,2048]{1,0:T(8,128)(2,1)} %bitcast.30, bf16[2048,2048]{1,0:T(8,128)(2,1)} %param.12), kind=kOutput, calls=%fused_computation.47 | convolution fusion | flops 4294967296 | bytes 14680064 | tf_op jit(solution)/shard_map/dot_general | solution.py:27
  71.1 0.0 reduce-scatter.2.cloned.1.call-update
  71.1 0.7 copy-done.8
  71.9 0.2 fusion.6
  72.0 0.0 copy-done.6
  72.0 0.2 fusion.8
  72.2 0.0 copy-done
  72.2 1.4 fusion.10
  73.6 0.6 iota_add_fusion
  74.2 13.8 %all_gather.11 = bf16[64,4096]{1,0:T(8,128)(2,1)S(1)} all-gather(bf16[32,4096]{1,0:T(8,128)(2,1)} %param.19), channel_id=1, replica_groups=mesh['vocab'=16,'grp'=2] {'grp'}, dimensions={0}, use_global_device_ids=true | all-gather | bytes 786432 | tf_op jit(solution)/shard_map/all_gather | solution.py:43
  88.0 70.1 %all-reduce.4 = (bf16[256,256]{1,0:T(8,128)(2,1)}, bf16[256,64]{0,1:T(8,128)(2,1)S(1)}, bf16[256,1024]{1,0:T(8,128)(2,1)}) all-reduce(f32[256,256]{1,0:T(8,128)S(1)} %fusion.8, f32[256,64]{0,1:T(8,128)S(1)} %fusion.6, f32[256,1024]{1,0:T(8,128)} %fusion.10), channel_id=1, replica_groups=mesh['vocab'=16,'grp'=2] {'vocab'}, use_global_device_ids=true, to_apply=%region_4.5 | all-reduce | flops 344064 | bytes 2064384 | tf_op jit(solution)/shard_map/psum | solution.py:38
  158.1 0.0 copy-done.9
  158.1 0.0 copy-done.7
  158.1 0.7 fusion.18
  158.8 0.0 copy-start.12
  158.8 2.7 fusion.21
  161.5 0.0 copy-done.12
  161.5 7.7 %fusion.20 = f32[256,4096]{1,0:T(8,128)} fusion(bf16[256,1024]{1,0:T(8,128)(2,1)S(1)} %copy-done.12, bf16[1024,4096]{1,0:T(8,128)(2,1)} %all-gather.3.cloned.1.call-done), kind=kOutput, calls=%fused_computation.48 | convolution fusion | flops 2147483648 | bytes 13107200 | tf_op jit(solution)/shard_map/dot_general | solution.py:47
  169.2 3.7 %all-gather.5.cloned.1.call-done = bf16[256,4096]{1,0:T(8,128)(2,1)} async-done(((bf16[128,4096]{1,0:T(8,128)(2,1)}), bf16[256,4096]{1,0:T(8,128)(2,1)}) %all-gather.5.cloned.1.call-update) | async-done | bytes 2097168 | tf_op jit(solution)/shard_map/all_gather | solution.py:42
  172.8 0.0 copy-done.10
  172.9 0.0 copy-done.13
  172.9 6.2 %select_reduce_fusion.1 = (f32[256]{0:T(256)S(1)}, f32[256]{0:T(256)S(1)}, f32[256]{0:T(256)S(1)}, f32[256,4096]{1,0:T(8,128)S(1)}) fusion(s32[4096]{0:T(1024)S(1)} %copy-done.10, s32[256]{0:T(256)S(1)} %multiply_subtract_fusion, pred[256]{0:T(512)(128)(4,1)S(1)} %get-tuple-element.24, f32[256,4096]{1,0:T(8,128)} %fusion.21, ...), kind=kOutput, calls=%fused_computation.9 | convolution fusion | flops 547355904 | bytes 14832384 | tf_op jit(solution)/shard_map/dot_general | solution.py:47
  179.0 0.0 copy-start.3
  179.1 1.9 copy-done.3
  181.0 0.0 copy-done.1
  181.0 0.0 copy-done.2
  181.0 0.8 fusion.1
  181.8 47.6 %reduce-scatter.2.cloned.1.call-done = f32[256,2048]{1,0:T(8,128)} async-done(((f32[512,2048]{1,0:T(8,128)}), f32[256,2048]{1,0:T(8,128)}) %reduce-scatter.2.cloned.1.call-update) | async-done | bytes 2097168 | tf_op jit(solution)/shard_map/reduce_scatter | solution.py:28
  229.5 1.8 reduce_max.28
  231.2 30.0 %all-reduce.2 = (f32[256]{0:T(256)S(1)}, f32[256,3]{0,1:T(4,128)S(1)}) all-reduce(f32[256]{0:T(256)S(1)} %reduce_max.28, f32[256,3]{0,1:T(4,128)S(1)} %bitcast.34), channel_id=1, replica_groups=mesh['vocab'=16,'grp'=2] {'vocab'}, use_global_device_ids=true, to_apply=%region_15.16 | all-reduce | flops 1024 | bytes 8192 | tf_op jit(solution)/shard_map/pmax | solution.py:67
  261.2 0.0 copy-start.11
  261.2 6.6 %multiply_reduce_fusion = (f32[3,256]{1,0:T(4,128)S(1)}, f32[3,256]{1,0:T(4,128)S(1)}) fusion(f32[3,256]{1,0:T(4,128)S(1)} %bitcast.31, f32[1,256,4096]{2,1,0:T(8,128)} %bitcast.23, f32[1,256,4096]{2,1,0:T(8,128)} %bitcast.28, f32[1,256,4096]{2,1,0:T(8,128)} %bitcast.25), kind=kLoop, calls=%fused_computation.1 | loop fusion | flops 18872832 | bytes 12592128 | tf_op jit(solution)/shard_map/reduce_sum | solution.py:71
  267.9 0.6 exponential_reduce_fusion
  268.5 57.0 %all-reduce = (f32[256]{0:T(256)S(1)}, f32[256,3]{0,1:T(4,128)S(1)}, f32[256]{0:T(256)S(1)}, f32[256,3]{0,1:T(4,128)S(1)}) all-reduce(f32[256]{0:T(256)S(1)} %add_add_fusion, f32[256,3]{0,1:T(4,128)S(1)} %bitcast.33, f32[256]{0:T(256)S(1)} %get-tuple-element.4, f32[256,3]{0,1:T(4,128)S(1)} %bitcast.32), channel_id=1, replica_groups=mesh['vocab'=16,'grp'=2] {'vocab'}, use_global_device_ids=true, to_apply=%region_8.9 | all-reduce | flops 2048 | bytes 16384 | tf_op jit(solution)/shard_map/psum | solution.py:72
  325.5 0.6 exponential_reduce_fusion.1
  326.1 0.6 fusion.14
  (18 shorter events, 0.1 us)
Async XLA Ops:
  7.2 65.1 %copy-start = (bf16[256,1024]{1,0:T(8,128)(2,1)S(1)}, bf16[256,1024]{1,0:T(8,128)(2,1)}, u32[]{:S(2)}) copy-start(bf16[256,1024]{1,0:T(8,128)(2,1)} %param.14) | copy-start | bytes 1572868
  7.2 1.6 copy-start.4
  7.2 154.3 %all-gather.3.cloned.1.call-start = ((), (), s32[]{:S(2)}) async-start(), calls=%async_computation.3 | async-start | bytes 12582912 | tf_op jit(solution)/shard_map/all_gather | solution.py:41
  11.3 45.3 %all-to-all-start = ((bf16[256,2,2048]{0,2,1:T(8,128)(2,1)}), bf16[256,2,2048]{0,2,1:T(8,128)(2,1)}, u32[]{:S(2)}, u32[]{:S(2)}) async-start(bf16[256,2,2048]{0,2,1:T(8,128)(2,1)} %bitcast.29), calls=%async_computation | async-start | bytes 4194304 | tf_op jit(solution)/shard_map/all_to_all | solution.py:26
  16.2 156.7 %all-gather.5.cloned.1.call-start = ((), (), s32[]{:S(2)}) async-start(), calls=%async_computation.4 | async-start | bytes 3145728 | tf_op jit(solution)/shard_map/all_gather | solution.py:42
  16.9 212.5 %reduce-scatter.2.cloned.1.call-start = ((), (), s32[]{:S(2)}) async-start(), calls=%async_computation.2 | async-start | bytes 6291456 | tf_op jit(solution)/shard_map/reduce_scatter | solution.py:28
  71.1 0.8 copy-start.8
  71.1 0.9 copy-start.6
  71.1 87.0 %copy-start.9 = (s32[256]{0:T(256)S(1)}, s32[256]{0:T(256)}, u32[]{:S(2)}) copy-start(s32[256]{0:T(256)} %param.20) | copy-start | bytes 3076
  71.1 87.0 %copy-start.7 = (bf16[4096,3]{0,1:T(4,128)(2,1)S(1)}, bf16[4096,3]{0,1:T(4,128)(2,1)}, u32[]{:S(2)}) copy-start(bf16[4096,3]{0,1:T(4,128)(2,1)} %param.13) | copy-start | bytes 73732
  158.8 2.7 copy-start.12
  161.5 11.4 %copy-start.10 = (s32[4096]{0:T(1024)S(1)}, s32[4096]{0:T(1024)}, u32[]{:S(2)}) copy-start(s32[4096]{0:T(1024)} %iota_add_fusion) | copy-start | bytes 49156
  161.5 11.4 %copy-start.13 = (bf16[256,256]{1,0:T(8,128)(2,1)S(1)}, bf16[256,256]{1,0:T(8,128)(2,1)}, u32[]{:S(2)}) copy-start(bf16[256,256]{1,0:T(8,128)(2,1)} %get-tuple-element.15) | copy-start | bytes 393220
  172.9 8.1 %copy-start.1 = (f32[256,4096]{1,0:T(8,128)S(1)}, f32[256,4096]{1,0:T(8,128)}, u32[]{:S(2)}) copy-start(f32[256,4096]{1,0:T(8,128)} %fusion.21) | copy-start | bytes 12582916
  172.9 8.1 %copy-start.2 = (f32[256,4096]{1,0:T(8,128)S(1)}, f32[256,4096]{1,0:T(8,128)}, u32[]{:S(2)}) copy-start(f32[256,4096]{1,0:T(8,128)} %fusion.20) | copy-start | bytes 12582916
  179.0 1.9 copy-start.3
  261.2 6.7 %copy-start.5 = (f32[256,2048]{1,0:T(8,128)S(1)}, f32[256,2048]{1,0:T(8,128)}, u32[]{:S(2)}) copy-start(f32[256,2048]{1,0:T(8,128)} %reduce-scatter.2.cloned.1.call-done) | copy-start | bytes 6291460
  261.2 64.3 %copy-start.11 = (s32[256,3]{0,1:T(4,128)S(1)}, s32[256,3]{0,1:T(4,128)}, u32[]{:S(2)}) copy-start(s32[256,3]{0,1:T(4,128)} %param.21) | copy-start | bytes 9220
Sparse Core Ops, SparseCore 0:
  9.6 128.1 all-gather.2
  139.3 33.4 all-gather.4
  175.1 54.2 reduce-scatter.1
where the time goes:
time: 339 us; the launch traced here: 333 us
  blocking collectives  171 us (50%)
  waiting for transfers between devices  92.3 us (27%)
  matrix products  29.4 us (9%)
  between operations  13.9 us (4%)
  other arithmetic  11.7 us (3%)
  local copies, waits for them, and re-layouts  10 us (3%)
  starting transfers between devices  5.02 us (1%)
    psum x1, blocking collectives, shards(): summed = lax.psum(partial_proj, 'vocab')  70.1 us
    psum x1, blocking collectives, shards(): lax.psum((head_sum, tail_sum, tail_weighted, picked), 'vocab')  57 us
    reduce_scatter x1, waiting for transfers between devices, shards(): lax.psum_scatter(partial_logits, 'grp', scatter_dimension=0, tiled=True)  47.6 us
    all_to_all x1, waiting for transfers between devices, shards(): lax.all_to_all(hidden, 'grp', split_axis=1, concat_axis=0, tiled=True)  39.6 us
    pmax x1, blocking collectives, shards(): head_max, tail_max = lax.pmax((local_head_max, local_tail_max), 'vocab')  30 us
    dot_general x3, matrix products, shards(): jnp.dot(projected[index], full_tails[index], preferred_element_type=jnp.f...  16.5 us
    all_gather x1, blocking collectives, shards(): lax.all_gather(tail_three, 'grp', axis=0, tiled=True)  13.8 us
    dot_general x1, matrix products, shards(): jnp.dot(every_row, head_weight, preferred_element_type=jnp.float32)  10.5 us
  transfers between devices with their start and end apart: 4, of which 3 were waited for; matrix products, arithmetic and copies ran while one was open for 11% of the time, Pallas kernels for 0%

commit v1 on v0

v1 whole, which is shorter than its diff:
```python
import functools

import jax
import jax.numpy as jnp
from jax import lax
from jax.experimental import pallas as pl
from jax.experimental.pallas import tpu as pltpu
from jax.sharding import PartitionSpec as P

MESH = pl.DeviceIdType.MESH
VMEM = pl.BlockSpec(memory_space=pltpu.VMEM)
F32 = jnp.float32
BF16 = jnp.bfloat16


def greet(nv, n, members, v, g):
    barrier = pltpu.get_barrier_semaphore()

    def one(d, carry):
        pl.semaphore_signal(barrier, inc=1, device_id=(peer(v, d, members), g), device_id_type=MESH)
        return carry

    lax.fori_loop(1, members, one, 0)
    for s in range(1, n):
        pl.semaphore_signal(barrier, inc=1, device_id=(v, lax.rem(g + s, n)), device_id_type=MESH)
    pl.semaphore_wait(barrier, members - 1 + n - 1)


def peer(v, d, members):
    base = (v // members) * members
    return base + lax.rem(v - base + d, members)


def spread(src, buf, slot, v, g, members, send, recv, landed):
    def copy(d):
        return pltpu.make_async_remote_copy(
            src_ref=src,
            dst_ref=landed(slot),
            send_sem=send.at[d],
            recv_sem=recv.at[d],
            device_id=(peer(v, d, members), g),
            device_id_type=MESH,
        )

    def arrival(d):
        from_slot = lax.rem(slot - d + members, members)
        return pltpu.make_async_remote_copy(
            src_ref=src,
            dst_ref=landed(from_slot),
            send_sem=send.at[d],
            recv_sem=recv.at[d],
            device_id=(peer(v, d, members), g),
            device_id_type=MESH,
        )

    def start(d, carry):
        copy(d).start()
        return carry

    def finish(d, carry):
        copy(d).wait_send()
        arrival(d).wait_recv()
        return carry

    lax.fori_loop(1, members, start, 0)
    return lambda: lax.fori_loop(1, members, finish, 0)


def across(src, dst, s, v, g, n, sign, send, recv):
    return pltpu.make_async_remote_copy(
        src_ref=src,
        dst_ref=dst,
        send_sem=send.at[s],
        recv_sem=recv.at[s],
        device_id=(v, lax.rem(g + sign * s + n, n)),
        device_id_type=MESH,
    )


def hidden_kernel(n, nv, members, piece_ref, out_ref, buf, ysend, yrecv, send, recv):
    v, g = lax.axis_index("vocab"), lax.axis_index("grp")
    slot = lax.rem(v, members)
    greet(nv, n, members, v, g)
    crossing = [
        across(piece_ref.at[s - 1], buf.at[s - 1, slot], s, v, g, n, 1, ysend, yrecv)
        for s in range(1, n)
    ]
    for copy in crossing:
        copy.start()
    waits = []
    for s in range(1, n):
        crossing[s - 1].wait_recv()
        waits.append(
            spread(
                buf.at[s - 1, slot], buf, slot, v, g, members,
                send.at[s - 1], recv.at[s - 1], lambda i, s=s: buf.at[s - 1, i],
            )
        )
    for s in range(1, n):
        crossing[s - 1].wait_send()
        waits[s - 1]()
    out_ref[...] = buf[...]


def exchange_hidden(pieces, n, nv, members):
    shape = (n - 1, members) + pieces.shape[1:]
    return pl.pallas_call(
        functools.partial(hidden_kernel, n, nv, members),
        out_shape=jax.ShapeDtypeStruct(shape, pieces.dtype),
        in_specs=[VMEM],
        out_specs=VMEM,
        scratch_shapes=[
            pltpu.VMEM(shape, pieces.dtype),
            pltpu.SemaphoreType.DMA((n,)),
            pltpu.SemaphoreType.DMA((n,)),
            pltpu.SemaphoreType.DMA((n - 1, members)),
            pltpu.SemaphoreType.DMA((n - 1, members)),
        ],
        compiler_params=pltpu.CompilerParams(
            collective_id=1, has_side_effects=True, vmem_limit_bytes=40 << 20
        ),
        name="hidden_exchange",
    )(pieces)


def proj_kernel(n, nv, part_ref, out_ref, mail, buf, ysend, yrecv, rsend, rrecv, send, recv):
    v, g = lax.axis_index("vocab"), lax.axis_index("grp")
    greet(nv, n, nv, v, g)

    def give(d):
        return pltpu.make_async_remote_copy(
            src_ref=part_ref.at[lax.rem(v + d, nv)],
            dst_ref=mail.at[d],
            send_sem=rsend.at[d],
            recv_sem=rrecv.at[d],
            device_id=(lax.rem(v + d, nv), g),
            device_id_type=MESH,
        )

    def start(d, carry):
        give(d).start()
        return carry

    lax.fori_loop(1, nv, start, 0)

    def add(d, total):
        give(d).wait()
        return total + mail[d].astype(F32)

    total = lax.fori_loop(1, nv, add, part_ref[v].astype(F32))
    buf[0, v] = total.astype(BF16)
    crossing = [across(buf.at[0, v], buf.at[s, v], s, v, g, n, 1, ysend, yrecv) for s in range(1, n)]
    for copy in crossing:
        copy.start()
    waits = []
    for s in range(n):
        if s:
            crossing[s - 1].wait_recv()
        waits.append(
            spread(
                buf.at[s, v], buf, v, v, g, nv, send.at[s], recv.at[s],
                lambda i, s=s: buf.at[s, i],
            )
        )
    for copy in crossing:
        copy.wait_send()
    for wait in waits:
        wait()
    out_ref[...] = buf[...]


def sum_projections(parts, n, nv):
    shape = (n,) + parts.shape
    return pl.pallas_call(
        functools.partial(proj_kernel, n, nv),
        out_shape=jax.ShapeDtypeStruct(shape, BF16),
        in_specs=[VMEM],
        out_specs=VMEM,
        scratch_shapes=[
            pltpu.VMEM(parts.shape, BF16),
            pltpu.VMEM(shape, BF16),
            pltpu.SemaphoreType.DMA((n,)),
            pltpu.SemaphoreType.DMA((n,)),
            pltpu.SemaphoreType.DMA((nv,)),
            pltpu.SemaphoreType.DMA((nv,)),
            pltpu.SemaphoreType.DMA((n, nv)),
            pltpu.SemaphoreType.DMA((n, nv)),
        ],
        compiler_params=pltpu.CompilerParams(
            collective_id=2, has_side_effects=True, vmem_limit_bytes=40 << 20
        ),
        name="projection_sum",
    )(parts)


def merge(blocks):
    rows = []
    for c in range(4):
        m, s, w, p = (blocks[:, 4 * c + i, :] for i in range(4))
        top = jnp.max(m, axis=0, keepdims=True)
        scale = jnp.exp(m - top)
        rows += [
            top,
            jnp.sum(s * scale, axis=0, keepdims=True),
            jnp.sum(w * scale, axis=0, keepdims=True),
            jnp.sum(p, axis=0, keepdims=True),
        ]
    return rows


def final_kernel(n, nv, v_head, tail, tail_ref, head_ref, clus_ref, tgt_ref, flag_ref, out_ref,
                 mail, buf, ysend, yrecv, send, recv):
    v, g = lax.axis_index("vocab"), lax.axis_index("grp")
    greet(nv, n, nv, v, g)
    crossing = [
        across(tail_ref.at[s], mail.at[s], s, v, g, n, -1, ysend, yrecv) for s in range(1, n)
    ]
    for copy in crossing:
        copy.start()
    mail[0] = tail_ref[0]
    for copy in crossing:
        copy.wait()
    rows = merge(mail[...])
    buf[v] = jnp.concatenate(rows[:12] + [head_ref[...]], axis=0)
    spread(buf.at[v], buf, v, v, g, nv, send, recv, lambda i: buf.at[i])()
    rows = merge(buf[...])
    clus = clus_ref[...]
    targets = tgt_ref[...]
    head_max, head_sum, _, picked = rows[12:]
    for c in range(3):
        picked = picked + rows[4 * c + 3]
    top = jnp.maximum(head_max, jnp.max(clus, axis=0, keepdims=True))
    total = head_sum * jnp.exp(head_max - top) + jnp.sum(jnp.exp(clus - top), axis=0, keepdims=True)
    head_lse = top + jnp.log(total)
    term = jnp.zeros_like(head_lse)
    out = []
    for c in range(3):
        lse = rows[4 * c] + jnp.log(rows[4 * c + 1])
        mean = rows[4 * c + 2] / rows[4 * c + 1]
        out.append(flag_ref[c : c + 1, :] * (lse - mean))
        low = v_head + c * tail
        inside = jnp.logical_and(targets >= low, targets < low + tail)
        term = term + jnp.where(inside, clus[c : c + 1, :] - lse, 0.0)
    out_ref[...] = jnp.concatenate([picked + term - head_lse] + out, axis=0)


def finish(tails, head, clus, targets, flags, n, nv, v_head, tail):
    rows = head.shape[1]
    return pl.pallas_call(
        functools.partial(final_kernel, n, nv, v_head, tail),
        out_shape=jax.ShapeDtypeStruct((4, rows), F32),
        in_specs=[VMEM] * 5,
        out_specs=VMEM,
        scratch_shapes=[
            pltpu.VMEM((n, 16, rows), F32),
            pltpu.VMEM((nv, 16, rows), F32),
            pltpu.SemaphoreType.DMA((n,)),
            pltpu.SemaphoreType.DMA((n,)),
            pltpu.SemaphoreType.DMA((nv,)),
            pltpu.SemaphoreType.DMA((nv,)),
        ],
        compiler_params=pltpu.CompilerParams(
            collective_id=3, has_side_effects=True, vmem_limit_bytes=40 << 20
        ),
        name="totals",
    )(tails, head, clus, targets, flags)


def stats_kernel(parts, tile, *refs):
    xs, ws = refs[:parts], refs[parts : 2 * parts]
    tgt_ref, out_ref, acc = refs[2 * parts :]
    step = pl.program_id(0)

    @pl.when(step == 0)
    def _():
        acc[:, 0:1] = jnp.full((acc.shape[0], 1), -jnp.inf, F32)
        acc[:, 1:] = jnp.zeros((acc.shape[0], acc.shape[1] - 1), F32)

    logits = jnp.dot(xs[0][...], ws[0][...], preferred_element_type=F32)
    for x, w in zip(xs[1:], ws[1:]):
        logits += jnp.dot(x[...], w[...], preferred_element_type=F32)
    before = acc[:, 0:1]
    top = jnp.maximum(before, jnp.max(logits, axis=1, keepdims=True))
    scale = jnp.exp(before - top)
    expo = jnp.exp(logits - top)
    ids = lax.broadcasted_iota(jnp.int32, logits.shape, 1) + step * tile
    acc[:, 0:1] = top
    acc[:, 1:2] = acc[:, 1:2] * scale + jnp.sum(expo, axis=1, keepdims=True)
    acc[:, 2:3] = acc[:, 2:3] * scale + jnp.sum(expo * logits, axis=1, keepdims=True)
    acc[:, 3:4] += jnp.sum(jnp.where(ids == tgt_ref[...], logits, 0.0), axis=1, keepdims=True)

    @pl.when(step == pl.num_programs(0) - 1)
    def _():
        out_ref[...] = acc[...].T[:8]


def softmax_stats(xs, ws, targets):
    rows, words = xs[0].shape[0], ws[0].shape[1]
    tile = min(512, words)
    depth = sum(w.shape[0] for w in ws)
    return pl.pallas_call(
        functools.partial(stats_kernel, len(xs), tile),
        grid=(words // tile,),
        out_shape=jax.ShapeDtypeStruct((8, rows), F32),
        in_specs=[pl.BlockSpec(x.shape, lambda i: (0, 0)) for x in xs]
        + [pl.BlockSpec((w.shape[0], tile), lambda i: (0, i)) for w in ws]
        + [pl.BlockSpec((rows, 1), lambda i: (0, 0))],
        out_specs=pl.BlockSpec((8, rows), lambda i: (0, 0)),
        scratch_shapes=[pltpu.VMEM((rows, 128), F32)],
        compiler_params=pltpu.CompilerParams(vmem_limit_bytes=40 << 20),
        cost_estimate=pl.CostEstimate(
            flops=2 * rows * words * depth + 20 * rows * words,
            bytes_accessed=2 * depth * (rows + words),
            transcendentals=rows * words,
        ),
        name="softmax_stats",
    )(*xs, *ws, targets)


def shards(
    n, nv, hidden, head_weight, cluster_weight, proj_one, proj_two, proj_three,
    tail_one, tail_two, tail_three, targets, flags,
):
    v, g = lax.axis_index("vocab"), lax.axis_index("grp")
    rows, width = hidden.shape
    depth = width // n
    head_cols, tail_cols = head_weight.shape[1], tail_one.shape[1]
    v_head, tail = head_cols * nv, tail_cols * nv
    share = tail_cols // n
    members = 4 if nv % 4 == 0 else 1

    def shift(value, s):
        return lax.ppermute(value, "grp", [(i, (i + s) % n) for i in range(n)])

    def columns(value, index, size):
        return lax.dynamic_slice_in_dim(value, index * size, size, 1)

    quarter = rows // members
    mine = lax.dynamic_slice_in_dim(hidden, lax.rem(v, members) * quarter, quarter, 0)
    pieces = jnp.stack([columns(mine, (g + s) % n, depth) for s in range(1, n)])
    others = exchange_hidden(pieces, n, nv, members).reshape(n - 1, rows, depth)

    two = [columns(tail_two, g, share)] + [shift(columns(tail_two, (g + s) % n, share), s) for s in range(1, n)]
    three = [columns(tail_three, g, share)] + [shift(columns(tail_three, (g + s) % n, share), s) for s in range(1, n)]
    one_src, others = lax.optimization_barrier((tail_one, others))
    one = [columns(one_src, g, share)] + [shift(columns(one_src, (g + s) % n, share), s) for s in range(1, n)]
    all_targets = jnp.concatenate([targets] + [shift(targets, s) for s in range(1, n)])

    sent = [jnp.dot(others[s - 1], head_weight, preferred_element_type=F32).astype(BF16) for s in range(1, n)]
    features = columns(hidden, v, proj_one.shape[0])
    parts = jnp.concatenate(
        [jnp.dot(features, w, preferred_element_type=F32).astype(BF16) for w in (proj_one, proj_two, proj_three)],
        axis=1,
    )
    sent, parts = lax.optimization_barrier((sent, parts))
    arrived = [shift(sent[s - 1], -s) for s in range(1, n)]
    own = jnp.dot(columns(hidden, g, depth), head_weight, preferred_element_type=F32)
    projected = sum_projections(parts.reshape(nv, rows // nv, -1), n, nv).reshape(n * rows, -1)

    def ordered(value, weight):
        size = weight.shape[0]
        return [columns(value, (g - s + n) % n, size) for s in range(n)]

    p1, p2 = proj_one.shape[1], proj_two.shape[1]
    proj = (projected[:, :p1], projected[:, p1 : p1 + p2], projected[:, p1 + p2 :])
    relative = all_targets - v_head
    cluster = relative // tail
    local = relative - cluster * tail - (v * tail_cols + g * share)
    marks = [jnp.where(cluster == c, local, -1)[:, None] for c in range(3)]

    def joined(value, weights, mark):
        x = jnp.concatenate(ordered(value, weights[0]), axis=1)
        return softmax_stats([x], [jnp.concatenate(weights, axis=0)], mark)

    stats_two = joined(proj[1], two, marks[1])
    stats_three = joined(proj[2], three, marks[2])
    stats_one = softmax_stats(ordered(proj[0], tail_one), one, marks[0])
    totals = jnp.concatenate([stats_one[:4], stats_two[:4], stats_three[:4], jnp.zeros((4, n * rows), F32)])
    totals = jnp.transpose(totals.reshape(16, n, rows), (1, 0, 2))

    logits = own
    for value in arrived:
        logits = logits + value.astype(F32)
    head_max = jnp.max(logits, axis=1)
    head_sum = jnp.sum(jnp.exp(logits - head_max[:, None]), axis=1)
    ids = v * head_cols + lax.broadcasted_iota(jnp.int32, logits.shape, 1)
    head_pick = jnp.sum(jnp.where(ids == targets[:, None], logits, 0.0), axis=1)
    head = jnp.stack([head_max, head_sum, jnp.zeros_like(head_sum), head_pick])
    clus = jnp.dot(hidden, cluster_weight, preferred_element_type=F32)

    out = finish(totals, head, clus.T, targets[None, :], flags.astype(F32).T, n, nv, v_head, tail)
    return out[0], out[1:].T


def solution(mesh):
    n, nv = mesh.shape["grp"], mesh.shape["vocab"]
    return jax.shard_map(
        functools.partial(shards, n, nv),
        mesh=mesh,
        in_specs=(
            P("grp", None),
            P("grp", "vocab"),
            P(),
            P("vocab", None),
            P("vocab", None),
            P("vocab", None),
            P("grp", "vocab"),
            P("grp", "vocab"),
            P("grp", "vocab"),
            P("grp"),
            P("grp", None),
        ),
        out_specs=(P("grp"), P("grp", None)),
        check_vma=False,
    )
```

time: 339 us -> 191 us (0.56); the launches traced: 333 us -> 190 us
  blocking collectives: 171 us -> 0 us
  Pallas kernels: 0 us -> 150 us
  waiting for transfers between devices: 92.3 us -> 0.01 us
  matrix products: 29.4 us -> 14.2 us
  between operations: 13.9 us -> 1.02 us
  other arithmetic: 11.7 us -> 5.63 us
  local copies, waits for them, and re-layouts: 10 us -> 14.1 us
    pallas_call x0 -> x6, Pallas kernels: none -> 150 us  [the longest x1 81.8 us: sum_projections(): pl.pallas_call(functools.partial(proj_kernel, n, nv), out_shape=jax.Shape...]
    psum x2 -> x0, blocking collectives: 127 us -> none  [the longest x1 70.1 us: shards(): summed = lax.psum(partial_proj, 'vocab')]
    reduce_scatter x1 -> x0, waiting for transfers between devices: 47.6 us -> none  [shards(): lax.psum_scatter(partial_logits, 'grp', scatter_dimension=0, tiled=True)]
    all_to_all x1 -> x0, waiting for transfers between devices: 39.6 us -> none  [shards(): lax.all_to_all(hidden, 'grp', split_axis=1, concat_axis=0, tiled=True)]
    pmax x1 -> x0, blocking collectives: 30 us -> none  [shards(): head_max, tail_max = lax.pmax((local_head_max, local_tail_max), 'vocab')]
    dot_general x8 -> x6, matrix products: 29.4 us -> 14.2 us  [the longest x1 6.82 us: shards(): jnp.dot(others[s - 1], head_weight, preferred_element_type=F32).astype(BF16)]
    all_gather x1 -> x0, blocking collectives: 13.8 us -> none  [shards(): lax.all_gather(tail_three, 'grp', axis=0, tiled=True)]
    reduce_sum x3 -> x1, other arithmetic: 7.84 us -> 0.62 us  [shards(): head_sum = jnp.sum(jnp.exp(logits - head_max[:, None]), axis=1)]
  transfers between devices with their start and end apart: 4 -> 5, of which waited for: 3 -> 0; matrix products, arithmetic and copies ran while one was open for 11% -> 16% of each run, Pallas kernels for 0% -> 66%
where the time goes in v1:
time: 191 us; the launch traced here: 190 us
  Pallas kernels  150 us (79%)
  matrix products  14.2 us (7%)
  local copies, waits for them, and re-layouts  14.1 us (7%)
  other arithmetic  5.63 us (3%)
  starting transfers between devices  5.13 us (3%)
    pallas_call x1, Pallas kernels, sum_projections(): pl.pallas_call(functools.partial(proj_kernel, n, nv), out_shape=jax.Shape...  81.8 us
    pallas_call x1, Pallas kernels, exchange_hidden(): pl.pallas_call(functools.partial(hidden_kernel, n, nv, members), out_shap...  29.7 us
    pallas_call x3, Pallas kernels, softmax_stats(): pl.pallas_call(functools.partial(stats_kernel, len(xs), tile), grid=(word...  23.9 us
    pallas_call x1, Pallas kernels, finish(): pl.pallas_call(functools.partial(final_kernel, n, nv, v_head, tail), out_...  15 us
    dot_general x1, matrix products, shards(): jnp.dot(others[s - 1], head_weight, preferred_element_type=F32).astype(BF16)  6.82 us
    dynamic_slice x6, local copies, waits for them, and re-layouts, columns(): return lax.dynamic_slice_in_dim(value, index * size, size, 1)  6.72 us
    dot_general x1, matrix products, shards(): jnp.dot(columns(hidden, g, depth), head_weight, preferred_element_type=F32)  6.05 us
    ppermute x5, starting transfers between devices, shift(): return lax.ppermute(value, 'grp', [(i, (i + s) % n) for i in range(n)])  5.13 us
  transfers between devices with their start and end apart: 5, of which 0 were waited for; matrix products, arithmetic and copies ran while one was open for 16% of the time, Pallas kernels for 66%

profile of v1, /device:TPU:1, one launch (start us, length us, event | category | flops | bytes accessed | tf_op | source)
XLA Modules:
  0.0 190.4 jit_solution(7625174172494380024)
XLA Ops:
  0.6 0.0 copy-start
  0.7 2.1 %collective-permute-start.1 = (s32[256]{0:T(256)}, s32[256]{0:T(256)S(1)}, u32[]{:S(2)}, u32[]{:S(2)}) collective-permute-start(s32[256]{0:T(256)} %param.20), channel_id=1, source_target_pairs={{0,1},{1,0},{2,3},{3,2},{4,5},{5,4},{6,7},{7,6},{8,9},{9,8},{10,11... | collective-permute-start | bytes 3080 | tf_op jit(solution)/shard_map/ppermute | solution.py:333
  2.8 1.7 constant_dynamic-slice_fusion.1
  4.5 0.2 collective-permute-start.3
  4.7 2.3 %constant_dynamic-slice_fusion.5 = (bf16[128,2048]{1,0:T(8,128)(2,1)}, bf16[128,2048]{1,0:T(8,128)(2,1)}) fusion(bf16[128,4096]{1,0:T(8,128)(2,1)} %param.18, s32[]{:T(128)S(6)} %select_n.131, s32[]{:T(128)S(6)} %select_n.125), kind=kLoop, calls=%fused_computation.44 | loop fusion | bytes 2097160 | tf_op jit(solution)/shard_map/dynamic_slice | solution.py:336
  7.0 1.3 collective-permute-start.2
  8.3 0.2 convolution_convert_fusion.3
  8.4 0.2 copy.25
  8.6 0.2 convolution_convert_fusion.2
  8.8 0.3 convolution_convert_fusion.1
  9.1 0.2 dynamic-slice_bitcast_fusion.piece_ref
  9.3 29.7 %hidden_exchange.1 = bf16[1,4,64,2048]{3,2,1,0:T(8,128)(2,1)S(1)} custom-call(bf16[1,64,2048]{2,1,0:T(8,128)(2,1)S(1)} %dynamic-slice_bitcast_fusion.piece_ref), custom_call_target="tpu_custom_call" | custom-call | tf_op jit(solution)/shard_map/hidden_exchange/pallas_call | solution.py:107
  38.9 0.0 copy-start.5
  39.0 6.8 %convolution_convert_fusion = bf16[256,2048]{1,0:T(8,128)(2,1)} fusion(bf16[2048,2048]{1,0:T(8,128)(2,1)} %param.12, bf16[1,256,2048]{2,1,0:T(8,128)(2,1)S(1)} %bitcast.38), kind=kOutput, calls=%fused_computation | convolution fusion | flops 2148007936 | bytes 10485760 | tf_op jit(solution)/shard_map/dot_general | solution.py:349
  45.8 0.1 pad_maximum_fusion.1
  45.8 1.0 collective-permute-start.4
  46.8 2.5 %constant_dynamic-slice_fusion.8 = (bf16[512,2048]{1,0:T(8,128)(2,1)}, bf16[512,2048]{1,0:T(8,128)(2,1)}) fusion(bf16[512,4096]{1,0:T(8,128)(2,1)S(1)} %copy-done.5, s32[]{:T(128)S(6)} %select_n.125, s32[]{:T(128)S(6)} %select_n.131), kind=kLoop, calls=%fused_computation.47 | loop fusion | bytes 8388616 | tf_op jit(solution)/shard_map/dynamic_slice | solution.py:336
  49.3 0.6 collective-permute-start
  49.8 81.8 %projection_sum.1 = bf16[2,16,16,1344]{3,2,1,0:T(8,128)(2,1)S(1)} custom-call(bf16[16,16,1344]{2,1,0:T(8,128)(2,1)S(1)} %bitcast.37), custom_call_target="tpu_custom_call" | custom-call | tf_op jit(solution)/shard_map/projection_sum/pallas_call | solution.py:174
  131.7 0.0 copy-start.13
  131.8 1.2 slice.32
  133.0 0.6 fusion.15.clus_ref
  133.8 0.1 constant_dynamic-slice_fusion.3
  133.9 1.0 copy-done.6
  134.9 0.1 constant_dynamic-slice_fusion.10
  135.0 0.1 pad_maximum_fusion.4.refs_0_
  135.1 0.6 iota_add_fusion
  135.7 0.6 pad.2.clone
  136.4 0.6 pad.7.clone
  137.0 0.6 copy-done.14
  137.5 0.7 pad_add_fusion
  138.2 0.9 copy.26
  139.1 1.2 compare_select_fusion.2
  140.3 1.0 pad_maximum_fusion.3.refs_1_
  141.3 6.3 %softmax_stats.5 = f32[8,512]{1,0:T(8,128)S(1)} custom-call(bf16[512,64]{1,0:T(8,128)(2,1)S(1)} %pad_maximum_fusion.4.refs_0_, bf16[64,2048]{1,0:T(8,128)(2,1)S(1)} %pad_maximum_fusion.3.refs_1_, s32[512,1]{1,0:T(8,128)S(1)} %get-tuple-element.19.refs_2_), custom_call_target="tpu_custom_call" | custom-call | flops 155189248 | bytes 327680 | tf_op jit(solution)/shard_map/softmax_stats/pallas_call | solution.py:301
  147.7 1.1 pad_maximum_fusion.refs_1_
  148.8 6.9 %softmax_stats.4 = f32[8,512]{1,0:T(8,128)S(1)} custom-call(bf16[512,256]{1,0:T(8,128)(2,1)S(1)} %pad_maximum_fusion.2.refs_0_, bf16[256,2048]{1,0:T(8,128)(2,1)S(1)} %pad_maximum_fusion.refs_1_, s32[512,1]{1,0:T(8,128)S(1)} %get-tuple-element.20.refs_2_), custom_call_target="tpu_custom_call" | custom-call | flops 557842432 | bytes 1310720 | tf_op jit(solution)/shard_map/softmax_stats/pallas_call | solution.py:301
  155.8 6.1 %fusion.14 = (f32[256]{0:T(256)S(1)}, f32[256,2048]{1,0:T(8,128)S(1)}) fusion(bf16[256,2048]{1,0:T(8,128)(2,1)} %collective-permute-done.4, bf16[2048,2048]{1,0:T(8,128)(2,1)} %param.12, bf16[256,4096]{1,0:T(8,128)(2,1)S(1)} %copy-done, s32[]{:T(128)S(6)} %select_n.131), kind=kOutput, calls=%fused_computation.53 | convolution fusion | flops 2149056256 | bytes 12583940 | tf_op jit(solution)/shard_map/dot_general | solution.py:357
  161.9 0.6 exponential_reduce_fusion
  162.5 0.0 copy-done.16
  162.5 0.1 pad_maximum_fusion.5.head_ref
  162.6 0.9 copy-done.1
  163.4 10.7 %softmax_stats.3 = f32[8,512]{1,0:T(8,128)S(1)} custom-call(bf16[512,512]{1,0:T(8,128)(2,1)S(1)} %get-tuple-element.15.refs_0_, bf16[512,512]{1,0:T(8,128)(2,1)S(1)} %get-tuple-element.14.refs_1_, bf16[512,2048]{1,0:T(8,128)(2,1)S(1)} %copy-done.1, bf16[512,2048]{1,0:T(8,128)(2,1)} %collective-permute-done.refs_3_, s32[512,1]{1,0:T(8,128)S(1)} %get-tuple-element.18.refs_4_), custom_call_target="tpu_custom_call" | custom-call | flops 2168455168 | bytes 5242880 | tf_op jit(solution)/shard_map/softmax_stats/pallas_call | solution.py:301
  174.1 0.0 slice-done.1
  174.2 0.1 maximum_maximum_fusion
  174.2 15.0 %totals.1 = f32[4,256]{1,0:T(4,128)S(1)} custom-call(f32[2,16,256]{2,1,0:T(8,128)S(1)} %bitcast.39, f32[4,256]{1,0:T(4,128)S(1)} %pad_maximum_fusion.5.head_ref, f32[3,256]{1,0:T(4,128)S(1)} %fusion.15.clus_ref, s32[1,256]{1,0:T(1,128)S(1)} %bitcast.41, f32[3,256]{1,0:T(4,128)S(1)} %convert_bitcast_fusion.flag_ref), custom_call_target="tpu_custom_call" | custom-call | tf_op jit(solution)/shard_map/totals/pallas_call | solution.py:249
  189.2 0.6 slice.30
  189.8 0.6 slice_bitcast_fusion
  (43 shorter events, 0.2 us)
Async XLA Ops:
  0.6 7.6 %copy-start = (bf16[256,4096]{1,0:T(8,128)(2,1)S(1)}, bf16[256,4096]{1,0:T(8,128)(2,1)}, u32[]{:S(2)}) copy-start(bf16[256,4096]{1,0:T(8,128)(2,1)} %param.11) | copy-start | bytes 6291460
  0.6 7.6 %copy-start.12 = (bf16[256,64]{0,1:T(8,128)(2,1)S(1)}, bf16[256,64]{0,1:T(8,128)(2,1)}, u32[]{:S(2)}) copy-start(bf16[256,64]{0,1:T(8,128)(2,1)} %param.16) | copy-start | bytes 98308
  0.7 7.9 %copy-start.9 = (bf16[256,256]{1,0:T(8,128)(2,1)S(1)}, bf16[256,256]{1,0:T(8,128)(2,1)}, u32[]{:S(2)}) copy-start(bf16[256,256]{1,0:T(8,128)(2,1)} %param.15) | copy-start | bytes 393220
  0.7 8.1 %copy-start.8 = (bf16[256,1024]{1,0:T(8,128)(2,1)S(1)}, bf16[256,1024]{1,0:T(8,128)(2,1)}, u32[]{:S(2)}) copy-start(bf16[256,1024]{1,0:T(8,128)(2,1)} %param.14) | copy-start | bytes 1572868
  0.7 136.3 %collective-permute-start.1 = (s32[256]{0:T(256)}, s32[256]{0:T(256)S(1)}, u32[]{:S(2)}, u32[]{:S(2)}) collective-permute-start(s32[256]{0:T(256)} %param.20), channel_id=1, source_target_pairs={{0,1},{1,0},{2,3},{3,2},{4,5},{5,4},{6,7},{7,6},{8,9},{9,8},{10,11... | collective-permute-start | bytes 3080 | tf_op jit(solution)/shard_map/ppermute | solution.py:333
  4.5 135.8 %collective-permute-start.3 = (bf16[32,2048]{1,0:T(8,128)(2,1)}, bf16[32,2048]{1,0:T(8,128)(2,1)}, u32[]{:S(2)}, u32[]{:S(2)}) collective-permute-start(bf16[32,2048]{1,0:T(8,128)(2,1)} %get-tuple-element.24), channel_id=1, source_target_pairs={{0,1},{1,0},{2,3},{3,2},{4,5},{5,4},{6,7},{7,6},{8,9},{9,8},{10,11... | collective-permute-start | bytes 393224 | tf_op jit(solution)/shard_map/ppermute | solution.py:333
  7.0 140.7 %collective-permute-start.2 = (bf16[128,2048]{1,0:T(8,128)(2,1)}, bf16[128,2048]{1,0:T(8,128)(2,1)}, u32[]{:S(2)}, u32[]{:S(2)}) collective-permute-start(bf16[128,2048]{1,0:T(8,128)(2,1)} %get-tuple-element.17), channel_id=1, source_target_pairs={{0,1},{1,0},{2,3},{3,2},{4,5},{5,4},{6,7},{7,6},{8,9},{9,8},{10,11... | collective-permute-start | bytes 1572872 | tf_op jit(solution)/shard_map/ppermute | solution.py:333
  38.9 7.9 %copy-start.5 = (bf16[512,4096]{1,0:T(8,128)(2,1)S(1)}, bf16[512,4096]{1,0:T(8,128)(2,1)}, u32[]{:S(2)}) copy-start(bf16[512,4096]{1,0:T(8,128)(2,1)} %param.17) | copy-start | bytes 12582916
  45.8 109.9 %collective-permute-start.4 = (bf16[256,2048]{1,0:T(8,128)(2,1)}, bf16[256,2048]{1,0:T(8,128)(2,1)}, u32[]{:S(2)}, u32[]{:S(2)}) collective-permute-start(bf16[256,2048]{1,0:T(8,128)(2,1)} %convolution_convert_fusion), channel_id=1, source_target_pairs={{0,1},{1,0},{2,3},{3,2},{4,5},{5,4},{6,7},{7,6},{8,9},{9,8},{10,11... | collective-permute-start | bytes 3145736 | tf_op jit(solution)/shard_map/ppermute | solution.py:333
  49.3 113.3 %collective-permute-start = (bf16[512,2048]{1,0:T(8,128)(2,1)}, bf16[512,2048]{1,0:T(8,128)(2,1)}, u32[]{:S(2)}, u32[]{:S(2)}) collective-permute-start(bf16[512,2048]{1,0:T(8,128)(2,1)} %get-tuple-element.12), channel_id=1, source_target_pairs={{0,1},{1,0},{2,3},{3,2},{4,5},{5,4},{6,7},{7,6},{8,9},{9,8},{10,11... | collective-permute-start | bytes 6291464 | tf_op jit(solution)/shard_map/ppermute | solution.py:333
  49.8 83.1 %copy-start.10 = (bf16[4096,3]{0,1:T(4,128)(2,1)S(1)}, bf16[4096,3]{0,1:T(4,128)(2,1)}, u32[]{:S(2)}) copy-start(bf16[4096,3]{0,1:T(4,128)(2,1)} %param.13) | copy-start | bytes 73732
  131.7 1.9 copy-start.13
  133.6 3.9 %copy-start.2 = (s32[256]{0:T(256)S(1)}, s32[256]{0:T(256)}, u32[]{:S(2)}) copy-start(s32[256]{0:T(256)} %param.20) | copy-start | bytes 3076
  133.7 1.2 copy-start.6
  137.0 0.6 copy-start.14
  139.1 8.6 %copy-start.7 = (bf16[128,2048]{1,0:T(8,128)(2,1)S(1)}, bf16[128,2048]{1,0:T(8,128)(2,1)}, u32[]{:S(2)}) copy-start(bf16[128,2048]{1,0:T(8,128)(2,1)} %get-tuple-element.16) | copy-start | bytes 1572868
  147.6 8.1 %copy-start.3 = (f32[8,512]{1,0:T(8,128)}, f32[8,512]{1,0:T(8,128)S(1)}, u32[]{:S(2)}) copy-start(f32[8,512]{1,0:T(8,128)S(1)} %softmax_stats.5) | copy-start | bytes 49156
  155.7 6.1 %copy-start.4 = (f32[8,512]{1,0:T(8,128)}, f32[8,512]{1,0:T(8,128)S(1)}, u32[]{:S(2)}) copy-start(f32[8,512]{1,0:T(8,128)S(1)} %softmax_stats.4) | copy-start | bytes 49156
  155.8 6.1 %copy-start.11 = (s32[2048]{0:T(1024)S(1)}, s32[2048]{0:T(1024)}, u32[]{:S(2)}) copy-start(s32[2048]{0:T(1024)} %iota_add_fusion) | copy-start | bytes 24580
  161.8 0.7 copy-start.16
  161.8 1.6 copy-start.1
  163.4 10.7 %slice-start = ((f32[8,512]{1,0:T(8,128)}), f32[4,512]{1,0:T(4,128)S(1)}, s32[]{:S(2)}) async-start(f32[8,512]{1,0:T(8,128)} %copy-done.3), calls=%async_computation | async-start | bytes 16384 | tf_op jit(solution)/shard_map/slice | solution.py:378
  163.4 10.7 %slice-start.1 = ((f32[8,512]{1,0:T(8,128)}), f32[4,512]{1,0:T(4,128)S(1)}, s32[]{:S(2)}) async-start(f32[8,512]{1,0:T(8,128)} %copy-done.4), calls=%async_computation.1 | async-start | bytes 16384 | tf_op jit(solution)/shard_map/slice | solution.py:378
  163.4 10.7 %copy-start.15 = (f32[16]{0:T(128)S(1)}, f32[16]{0:T(128)}, u32[]{:S(2)}) copy-start(f32[16]{0:T(128)} %pad.7.clone) | copy-start | bytes 196

commit v2 on v1

--- a/solution.py
+++ b/solution.py
@@ -77,54 +77,10 @@
     )
 
 
-def hidden_kernel(n, nv, members, piece_ref, out_ref, buf, ysend, yrecv, send, recv):
+def front_kernel(n, nv, members, piece_ref, part_ref, hid_ref, out_ref, hid, mail, buf,
+                 ysend, yrecv, rsend, rrecv, send, recv):
     v, g = lax.axis_index("vocab"), lax.axis_index("grp")
     slot = lax.rem(v, members)
-    greet(nv, n, members, v, g)
-    crossing = [
-        across(piece_ref.at[s - 1], buf.at[s - 1, slot], s, v, g, n, 1, ysend, yrecv)
-        for s in range(1, n)
-    ]
-    for copy in crossing:
-        copy.start()
-    waits = []
-    for s in range(1, n):
-        crossing[s - 1].wait_recv()
-        waits.append(
-            spread(
-                buf.at[s - 1, slot], buf, slot, v, g, members,
-                send.at[s - 1], recv.at[s - 1], lambda i, s=s: buf.at[s - 1, i],
-            )
-        )
-    for s in range(1, n):
-        crossing[s - 1].wait_send()
-        waits[s - 1]()
-    out_ref[...] = buf[...]
-
-
-def exchange_hidden(pieces, n, nv, members):
-    shape = (n - 1, members) + pieces.shape[1:]
-    return pl.pallas_call(
-        functools.partial(hidden_kernel, n, nv, members),
-        out_shape=jax.ShapeDtypeStruct(shape, pieces.dtype),
-        in_specs=[VMEM],
-        out_specs=VMEM,
-        scratch_shapes=[
-            pltpu.VMEM(shape, pieces.dtype),
-            pltpu.SemaphoreType.DMA((n,)),
-            pltpu.SemaphoreType.DMA((n,)),
-            pltpu.SemaphoreType.DMA((n - 1, members)),
-            pltpu.SemaphoreType.DMA((n - 1, members)),
-        ],
-        compiler_params=pltpu.CompilerParams(
-            collective_id=1, has_side_effects=True, vmem_limit_bytes=40 << 20
-        ),
-        name="hidden_exchange",
-    )(pieces)
-
-
-def proj_kernel(n, nv, part_ref, out_ref, mail, buf, ysend, yrecv, rsend, rrecv, send, recv):
-    v, g = lax.axis_index("vocab"), lax.axis_index("grp")
     greet(nv, n, nv, v, g)
 
     def give(d):
@@ -142,55 +98,163 @@
         return carry
 
     lax.fori_loop(1, nv, start, 0)
+    waits = [
+        spread(
+            piece_ref.at[s - 1], hid, slot, v, g, members,
+            send.at[s - 1], recv.at[s - 1], lambda i, s=s: hid.at[s - 1, i],
+        )
+        for s in range(1, n)
+    ]
+    for s in range(1, n):
+        hid[s - 1, slot] = piece_ref[s - 1]
 
     def add(d, total):
         give(d).wait()
         return total + mail[d].astype(F32)
 
     total = lax.fori_loop(1, nv, add, part_ref[v].astype(F32))
-    buf[0, v] = total.astype(BF16)
-    crossing = [across(buf.at[0, v], buf.at[s, v], s, v, g, n, 1, ysend, yrecv) for s in range(1, n)]
+    buf[0] = total.astype(BF16)
+    crossing = [across(buf.at[0], buf.at[s], s, v, g, n, 1, ysend, yrecv) for s in range(1, n)]
     for copy in crossing:
         copy.start()
-    waits = []
-    for s in range(n):
-        if s:
-            crossing[s - 1].wait_recv()
-        waits.append(
-            spread(
-                buf.at[s, v], buf, v, v, g, nv, send.at[s], recv.at[s],
-                lambda i, s=s: buf.at[s, i],
-            )
-        )
-    for copy in crossing:
-        copy.wait_send()
     for wait in waits:
         wait()
+    hid_ref[...] = hid[...]
+    for copy in crossing:
+        copy.wait()
     out_ref[...] = buf[...]
 
 
-def sum_projections(parts, n, nv):
-    shape = (n,) + parts.shape
+def front(pieces, parts, n, nv, members):
+    shape = (n - 1, members) + pieces.shape[1:]
+    block = (n,) + parts.shape[1:]
     return pl.pallas_call(
-        functools.partial(proj_kernel, n, nv),
-        out_shape=jax.ShapeDtypeStruct(shape, BF16),
-        in_specs=[VMEM],
-        out_specs=VMEM,
+        functools.partial(front_kernel, n, nv, members),
+        out_shape=(jax.ShapeDtypeStruct(shape, BF16), jax.ShapeDtypeStruct(block, BF16)),
+        in_specs=[VMEM] * 2,
+        out_specs=(VMEM, VMEM),
         scratch_shapes=[
+            pltpu.VMEM(shape, BF16),
             pltpu.VMEM(parts.shape, BF16),
-            pltpu.VMEM(shape, BF16),
+            pltpu.VMEM(block, BF16),
             pltpu.SemaphoreType.DMA((n,)),
             pltpu.SemaphoreType.DMA((n,)),
             pltpu.SemaphoreType.DMA((nv,)),
             pltpu.SemaphoreType.DMA((nv,)),
-            pltpu.SemaphoreType.DMA((n, nv)),
-            pltpu.SemaphoreType.DMA((n, nv)),
+            pltpu.SemaphoreType.DMA((n - 1, members)),
+            pltpu.SemaphoreType.DMA((n - 1, members)),
+        ],
+        compiler_params=pltpu.CompilerParams(
+            collective_id=1, has_side_effects=True, vmem_limit_bytes=40 << 20
+        ),
+        cost_estimate=pl.CostEstimate(flops=25 * 10**9, bytes_accessed=10**6, transcendentals=0),
+        name="front",
+    )(pieces, parts)
+
+
+def gather_kernel(nv, members, block_ref, after_ref, out_ref, buf, zsend, zrecv, send, recv):
+    v, g = lax.axis_index("vocab"), lax.axis_index("grp")
+    slot = lax.rem(v, members)
+    base = v - slot
+    levels = nv // members
+    barrier = pltpu.get_barrier_semaphore()
+
+    def far(d):
+        return lax.rem(v + d * members, nv)
+
+    def greet_far(d, carry):
+        pl.semaphore_signal(barrier, inc=1, device_id=(far(d), g), device_id_type=MESH)
+        return carry
+
+    def greet_near(d, carry):
+        pl.semaphore_signal(barrier, inc=1, device_id=(peer(v, d, members), g), device_id_type=MESH)
+        return carry
+
+    lax.fori_loop(1, levels, greet_far, 0)
+    lax.fori_loop(1, members, greet_near, 0)
+    pl.semaphore_wait(barrier, levels - 1 + members - 1)
+    buf[v] = block_ref[...]
+
+    def hop(d, landed):
+        return pltpu.make_async_remote_copy(
+            src_ref=buf.at[v],
+            dst_ref=buf.at[landed],
+            send_sem=zsend.at[d],
+            recv_sem=zrecv.at[d],
+            device_id=(far(d), g),
+            device_id_type=MESH,
+        )
+
+    def origin(owner, d):
+        return lax.rem(owner - d * members + nv, nv)
+
+    def near(d, e, landed):
+        return pltpu.make_async_remote_copy(
+            src_ref=buf.at[origin(v, d)],
+            dst_ref=buf.at[landed],
+            send_sem=send.at[d, e],
+            recv_sem=recv.at[d, e],
+            device_id=(peer(v, e, members), g),
+            device_id_type=MESH,
+        )
+
+    def start_far(d, carry):
+        hop(d, v).start()
+        return carry
+
+    def forward(d, carry):
+        def one(e, inner):
+            near(d, e, origin(v, d)).start()
+            return inner
+
+        return lax.fori_loop(1, members, one, carry)
+
+    def relay(d, carry):
+        hop(d, origin(v, d)).wait_recv()
+        return forward(d, carry)
+
+    def drain(d, carry):
+        def one(e, inner):
+            owner = base + lax.rem(slot - e + members, members)
+            near(d, e, origin(v, d)).wait_send()
+            near(d, e, origin(owner, d)).wait_recv()
+            return inner
+
+        return lax.fori_loop(1, members, one, carry)
+
+    def drain_far(d, carry):
+        hop(d, v).wait_send()
+        return carry
+
+    lax.fori_loop(1, levels, start_far, 0)
+    forward(0, 0)
+    lax.fori_loop(1, levels, relay, 0)
+    lax.fori_loop(0, levels, drain, 0)
+    lax.fori_loop(1, levels, drain_far, 0)
+    out_ref[...] = buf[...]
+
+
+def gather(block, begun, nv, members):
+    shape = (nv,) + block.shape
+    levels = nv // members
+    return pl.pallas_call(
+        functools.partial(gather_kernel, nv, members),
+        out_shape=jax.ShapeDtypeStruct(shape, BF16),
+        in_specs=[VMEM] * 2,
+        out_specs=VMEM,
+        scratch_shapes=[
+            pltpu.VMEM(shape, BF16),
+            pltpu.SemaphoreType.DMA((levels,)),
+            pltpu.SemaphoreType.DMA((levels,)),
+            pltpu.SemaphoreType.DMA((levels, members)),
+            pltpu.SemaphoreType.DMA((levels, members)),
         ],
         compiler_params=pltpu.CompilerParams(
             collective_id=2, has_side_effects=True, vmem_limit_bytes=40 << 20
         ),
-        name="projection_sum",
-    )(parts)
+        cost_estimate=pl.CostEstimate(flops=25 * 10**9, bytes_accessed=10**6, transcendentals=0),
+        name="projection_gather",
+    )(block, begun)
 
 
 def merge(blocks):
@@ -266,15 +330,18 @@
     )(tails, head, clus, targets, flags)
 
 
-def stats_kernel(parts, tile, *refs):
+def stats_kernel(parts, tile, last, *refs):
     xs, ws = refs[:parts], refs[parts : 2 * parts]
-    tgt_ref, out_ref, acc = refs[2 * parts :]
+    tgt_ref, out_ref, acc = refs[2 * parts], refs[-2], refs[-1]
     step = pl.program_id(0)
 
     @pl.when(step == 0)
     def _():
-        acc[:, 0:1] = jnp.full((acc.shape[0], 1), -jnp.inf, F32)
-        acc[:, 1:] = jnp.zeros((acc.shape[0], acc.shape[1] - 1), F32)
+        if len(refs) == 2 * parts + 4:
+            acc[...] = refs[2 * parts + 1][...]
+        else:
+            acc[:, 0:1] = jnp.full((acc.shape[0], 1), -jnp.inf, F32)
+            acc[:, 1:] = jnp.zeros((acc.shape[0], acc.shape[1] - 1), F32)
 
     logits = jnp.dot(xs[0][...], ws[0][...], preferred_element_type=F32)
     for x, w in zip(xs[1:], ws[1:]):
@@ -291,30 +358,27 @@
 
     @pl.when(step == pl.num_programs(0) - 1)
     def _():
-        out_ref[...] = acc[...].T[:8]
-
-
-def softmax_stats(xs, ws, targets):
+        out_ref[...] = acc[...].T[:8] if last else acc[...]
+
+
+def softmax_stats(xs, ws, targets, begun=(), last=True):
     rows, words = xs[0].shape[0], ws[0].shape[1]
-    tile = min(512, words)
-    depth = sum(w.shape[0] for w in ws)
+    tile = 512 if words % 512 == 0 else words
+    shape = (8, rows) if last else (rows, 128)
     return pl.pallas_call(
-        functools.partial(stats_kernel, len(xs), tile),
+        functools.partial(stats_kernel, len(xs), tile, last),
         grid=(words // tile,),
-        out_shape=jax.ShapeDtypeStruct((8, rows), F32),
+        out_shape=jax.ShapeDtypeStruct(shape, F32),
         in_specs=[pl.BlockSpec(x.shape, lambda i: (0, 0)) for x in xs]
         + [pl.BlockSpec((w.shape[0], tile), lambda i: (0, i)) for w in ws]
-        + [pl.BlockSpec((rows, 1), lambda i: (0, 0))],
-        out_specs=pl.BlockSpec((8, rows), lambda i: (0, 0)),
+        + [pl.BlockSpec((rows, 1), lambda i: (0, 0))]
+        + [pl.BlockSpec((rows, 128), lambda i: (0, 0)) for _ in begun],
+        out_specs=pl.BlockSpec(shape, lambda i: (0, 0)),
         scratch_shapes=[pltpu.VMEM((rows, 128), F32)],
         compiler_params=pltpu.CompilerParams(vmem_limit_bytes=40 << 20),
-        cost_estimate=pl.CostEstimate(
-            flops=2 * rows * words * depth + 20 * rows * words,
-            bytes_accessed=2 * depth * (rows + words),
-            transcendentals=rows * words,
-        ),
+        cost_estimate=pl.CostEstimate(flops=rows, bytes_accessed=rows, transcendentals=0),
         name="softmax_stats",
-    )(*xs, *ws, targets)
+    )(*xs, *ws, targets, *begun)
 
 
 def shards(
@@ -335,27 +399,53 @@
     def columns(value, index, size):
         return lax.dynamic_slice_in_dim(value, index * size, size, 1)
 
+    def cut(value, index, first, size):
+        return lax.dynamic_slice_in_dim(value, index * share + first, size, 1)
+
+    def swapped(value, first, size, later=0):
+        return [cut(value, g, first, size)] + [
+            shift(cut(value, (g + s) % n, first + later, size), s) for s in range(1, n)
+        ]
+
+    def after(value):
+        return (value[(0,) * value.ndim].astype(F32) > 1e30).astype(jnp.int32)
+
     quarter = rows // members
     mine = lax.dynamic_slice_in_dim(hidden, lax.rem(v, members) * quarter, quarter, 0)
-    pieces = jnp.stack([columns(mine, (g + s) % n, depth) for s in range(1, n)])
-    others = exchange_hidden(pieces, n, nv, members).reshape(n - 1, rows, depth)
-
-    two = [columns(tail_two, g, share)] + [shift(columns(tail_two, (g + s) % n, share), s) for s in range(1, n)]
-    three = [columns(tail_three, g, share)] + [shift(columns(tail_three, (g + s) % n, share), s) for s in range(1, n)]
-    one_src, others = lax.optimization_barrier((tail_one, others))
-    one = [columns(one_src, g, share)] + [shift(columns(one_src, (g + s) % n, share), s) for s in range(1, n)]
-    all_targets = jnp.concatenate([targets] + [shift(targets, s) for s in range(1, n)])
-
-    sent = [jnp.dot(others[s - 1], head_weight, preferred_element_type=F32).astype(BF16) for s in range(1, n)]
+    pieces = jnp.stack([shift(columns(mine, (g + s) % n, depth), s) for s in range(1, n)])
+
+    split = tail_two.shape[0]
+    small = [shift(jnp.concatenate([cut(t, (g + s) % n, 0, share) for t in (tail_two, tail_three)]), s) for s in range(1, n)]
+    bounds = (0, share // 4, share // 4 * 3, share) if share % 512 == 0 else (0, share)
+    spans = [(low, high - low) for low, high in zip(bounds, bounds[1:])]
+    one = [swapped(tail_one, *spans[0])]
+    away_targets = [shift(targets, s) for s in range(1, n)]
+
     features = columns(hidden, v, proj_one.shape[0])
     parts = jnp.concatenate(
         [jnp.dot(features, w, preferred_element_type=F32).astype(BF16) for w in (proj_one, proj_two, proj_three)],
         axis=1,
     )
-    sent, parts = lax.optimization_barrier((sent, parts))
+    others, block = front(pieces, parts.reshape(nv, rows // nv, -1), n, nv, members)
+    others = others.reshape(n - 1, rows, depth)
+
+    later = after(block)
+    for span in spans[1:2]:
+        one.append(swapped(tail_one, *span, later))
+    sent = [jnp.dot(others[s - 1], head_weight, preferred_element_type=F32).astype(BF16) for s in range(1, n)]
     arrived = [shift(sent[s - 1], -s) for s in range(1, n)]
+    later = after(sent[0])
+    for span in spans[2:]:
+        one.append(swapped(tail_one, *span, later))
     own = jnp.dot(columns(hidden, g, depth), head_weight, preferred_element_type=F32)
-    projected = sum_projections(parts.reshape(nv, rows // nv, -1), n, nv).reshape(n * rows, -1)
+    projected = gather(block, sent[0][:16, :128], nv, members)
+    later = after(projected)
+    two, three = (
+        [cut(t, g, 0, share)] + [lax.dynamic_slice_in_dim(w, low + later, t.shape[0], 0) for w in small]
+        for t, low in ((tail_two, 0), (tail_three, split))
+    )
+    all_targets = jnp.concatenate([targets] + [t + later for t in away_targets])
+    projected = jnp.transpose(projected, (1, 0, 2, 3)).reshape(n * rows, -1)
 
     def ordered(value, weight):
         size = weight.shape[0]
@@ -374,7 +464,10 @@
 
     stats_two = joined(proj[1], two, marks[1])
     stats_three = joined(proj[2], three, marks[2])
-    stats_one = softmax_stats(ordered(proj[0], tail_one), one, marks[0])
+    ones, begun = ordered(proj[0], tail_one), ()
+    for (low, _), words in zip(spans[:-1], one[:-1]):
+        begun = (softmax_stats(ones, words, marks[0] - low, begun, False),)
+    stats_one = softmax_stats(ones, one[-1], marks[0] - spans[-1][0], begun)
     totals = jnp.concatenate([stats_one[:4], stats_two[:4], stats_three[:4], jnp.zeros((4, n * rows), F32)])
     totals = jnp.transpose(totals.reshape(16, n, rows), (1, 0, 2))
 

time: 191 us -> 156 us (0.82)
  Pallas kernels: 150 us -> 84.8 us
  waiting for transfers between devices: 0.01 us -> 18.3 us
  local copies, waits for them, and re-layouts: 14.1 us -> 23.6 us
  between operations: 1.02 us -> 3.04 us
    pallas_call x5 -> x7, Pallas kernels: 135 us -> 73.5 us  [the longest x1 26.4 us: front(): pl.pallas_call(functools.partial(front_kernel, n, nv, members), out_shape...]
    ppermute x5 -> x7, waiting for transfers between devices: 0.01 us -> 18.3 us  [shift(): return lax.ppermute(value, 'grp', [(i, (i + s) % n) for i in range(n)])]
    dynamic_slice x0 -> x6, local copies, waits for them, and re-layouts: none -> 12.5 us  [the longest x4 10.3 us: cut(): return lax.dynamic_slice_in_dim(value, index * share + first, size, 1)]
    dynamic_slice x6 -> x4, local copies, waits for them, and re-layouts: 6.72 us -> 2.79 us  [columns(): return lax.dynamic_slice_in_dim(value, index * size, size, 1)]
    pallas_call x1, Pallas kernels: 15 us -> 11.3 us  [finish(): pl.pallas_call(functools.partial(final_kernel, n, nv, v_head, tail), out_...]
    slice x0 -> x4, local copies, waits for them, and re-layouts: none -> 2.9 us  [the longest x3 2.22 us: after(): return (value[(0,) * value.ndim].astype(F32) > 1e+30).astype(jnp.int32)]
    unnamed x34 -> x36, local copies, waits for them, and re-layouts: 2.5 us -> 0.09 us
    concatenate x2, other arithmetic: 2.13 us -> 0.12 us  [joined(): return softmax_stats([x], [jnp.concatenate(weights, axis=0)], mark)]
  transfers between devices with their start and end apart: 5 -> 7, of which waited for: 0 -> 1; matrix products, arithmetic and copies ran while one was open for 16% -> 23% of each run, Pallas kernels for 66% -> 47%
where the time goes in v2:
time: 156 us
  Pallas kernels  84.8 us (54%)
  local copies, waits for them, and re-layouts  23.6 us (15%)
  waiting for transfers between devices  18.3 us (12%)
  matrix products  14.7 us (9%)
  starting transfers between devices  6.43 us (4%)
  other arithmetic  4.79 us (3%)
  between operations  3.04 us (2%)
    pallas_call x1, Pallas kernels, front(): pl.pallas_call(functools.partial(front_kernel, n, nv, members), out_shape...  26.4 us
    pallas_call x5, Pallas kernels, softmax_stats(): pl.pallas_call(functools.partial(stats_kernel, len(xs), tile, last), grid...  26.3 us
    pallas_call x1, Pallas kernels, gather(): pl.pallas_call(functools.partial(gather_kernel, nv, members), out_shape=j...  20.8 us
    ppermute x7, waiting for transfers between devices, shift(): return lax.ppermute(value, 'grp', [(i, (i + s) % n) for i in range(n)])  18.3 us
    pallas_call x1, Pallas kernels, finish(): pl.pallas_call(functools.partial(final_kernel, n, nv, v_head, tail), out_...  11.3 us
    dynamic_slice x4, local copies, waits for them, and re-layouts, cut(): return lax.dynamic_slice_in_dim(value, index * share + first, size, 1)  10.3 us
    dot_general x1, matrix products, shards(): jnp.dot(others[s - 1], head_weight, preferred_element_type=F32).astype(BF16)  6.7 us
    ppermute x7, starting transfers between devices, shift(): return lax.ppermute(value, 'grp', [(i, (i + s) % n) for i in range(n)])  6.43 us
  transfers between devices with their start and end apart: 7, of which 1 were waited for; matrix products, arithmetic and copies ran while one was open for 23% of the time, Pallas kernels for 47%

profile of v2, /device:TPU:1, one launch (start us, length us, event | category | flops | bytes accessed | tf_op | source)
XLA Modules:
  0.0 155.6 jit_solution(7253647474144413170)
XLA Ops:
  0.6 2.1 %collective-permute-start.2 = (s32[256]{0:T(256)}, s32[256]{0:T(256)S(1)}, u32[]{:S(2)}, u32[]{:S(2)}) collective-permute-start(s32[256]{0:T(256)} %param.20), channel_id=1, source_target_pairs={{0,1},{1,0},{2,3},{3,2},{4,5},{5,4},{6,7},{7,6},{8,9},{9,8},{10,11... | collective-permute-start | bytes 3080 | tf_op jit(solution)/shard_map/ppermute | solution.py:397
  2.8 1.8 %dynamic_slice.64 = bf16[64,2048]{1,0:T(8,128)(2,1)} dynamic-slice(bf16[256,4096]{1,0:T(8,128)(2,1)} %param.11, s32[]{:T(128)S(6)} %select_n.161, s32[]{:T(128)S(6)} %select_n.164), dynamic_slice_sizes={64,2048} | dynamic-slice | bytes 524292 | tf_op jit(solution)/shard_map/dynamic_slice | solution.py:400
  4.7 1.8 %constant_dynamic-slice_fusion.1 = (bf16[32,2048]{1,0:T(8,128)(2,1)}, bf16[32,2048]{1,0:T(8,128)(2,1)S(1)}) fusion(bf16[32,4096]{1,0:T(8,128)(2,1)} %param.19, s32[]{:T(128)S(6)} %select_n.175, s32[]{:T(128)S(6)} %select_n.163), kind=kLoop, calls=%fused_computation.38 | loop fusion | bytes 524296 | tf_op jit(solution)/shard_map/dynamic_slice | solution.py:403
  6.5 2.1 %constant_dynamic-slice_fusion.7 = (bf16[128,2048]{1,0:T(8,128)(2,1)}, bf16[128,2048]{1,0:T(8,128)(2,1)S(1)}) fusion(bf16[128,4096]{1,0:T(8,128)(2,1)} %param.18, s32[]{:T(128)S(6)} %select_n.175, s32[]{:T(128)S(6)} %select_n.163), kind=kLoop, calls=%fused_computation.44 | loop fusion | bytes 2097160 | tf_op jit(solution)/shard_map/dynamic_slice | solution.py:403
  8.6 0.9 pad_maximum_fusion.2
  9.5 1.2 collective-permute-start.5
  10.7 0.6 fusion.14.clus_ref
  11.4 0.8 convolution_convert_fusion.3
  12.2 0.2 convolution_convert_fusion.2
  12.4 0.3 convolution_convert_fusion.1
  12.7 0.6 iota_add_fusion
  13.3 0.6 pad.2.clone
  13.9 0.6 pad.7.clone
  14.5 0.9 copy.28
  15.5 26.4 %front.1 = (bf16[1,4,64,2048]{3,2,1,0:T(8,128)(2,1)S(1)}, bf16[2,16,1344]{2,1,0:T(8,128)(2,1)S(1)}) custom-call(bf16[1,64,2048]{2,1,0:T(8,128)(2,1)S(1)} %bitcast.40, bf16[16,16,1344]{2,1,0:T(8,128)(2,1)S(1)} %bitcast.36), custom_call_target="tpu_custom_call" | custom-call | flops 24999999488 | bytes 1000000 | tf_op jit(solution)/shard_map/front/pallas_call | solution.py:131
  41.9 0.5 slice.40
  43.1 6.7 %convolution_convert_fusion = bf16[256,2048]{1,0:T(8,128)(2,1)} fusion(bf16[256,2048]{1,0:T(8,128)(2,1)S(1)} %bitcast.41, bf16[2048,2048]{1,0:T(8,128)(2,1)} %param.12), kind=kOutput, calls=%fused_computation | convolution fusion | flops 2148007936 | bytes 10485760 | tf_op jit(solution)/shard_map/dot_general | solution.py:435
  49.8 1.2 slice.50
  51.6 0.7 slice.48.after_ref
  52.3 0.4 collective-permute-start.6
  52.7 20.8 %projection_gather.1 = bf16[16,2,16,1344]{3,2,1,0:T(8,128)(2,1)S(1)} custom-call(bf16[2,16,1344]{2,1,0:T(8,128)(2,1)S(1)} %get-tuple-element.4.block_ref, bf16[16,128]{1,0:T(8,128)(2,1)S(1)} %slice.48.after_ref), custom_call_target="tpu_custom_call" | custom-call | flops 24999999488 | bytes 1000000 | tf_op jit(solution)/shard_map/projection_gather/pallas_call | solution.py:240
  73.5 0.5 slice.39
  74.0 0.1 copy.29
  74.2 1.1 slice.49
  75.9 3.1 %constant_dynamic-slice_fusion.10 = (bf16[512,512]{1,0:T(8,128)(2,1)}, bf16[512,512]{1,0:T(8,128)(2,1)}, bf16[512,512]{1,0:T(8,128)(2,1)S(1)}, bf16[512,512]{1,0:T(8,128)(2,1)}) fusion(bf16[512,4096]{1,0:T(8,128)(2,1)} %param.17, s32[]{:T(128)S(6)} %select_n.163, s32[]{:T(128)S(6)} %select_n.170, s32[]{:T(128)S(6)} %select_n.169, s32[]{:T(128)S(6)} %select_n.175), kind=kLoop, calls=%fused_computation.47 | loop fusion | bytes 4194320 | tf_op jit(solution)/shard_map/dynamic_slice | solution.py:403
  79.0 1.1 collective-permute-start.4
  80.2 0.3 collective-permute-start.1
  80.6 3.4 %constant_dynamic-slice_fusion.12 = (bf16[512,1024]{1,0:T(8,128)(2,1)}, bf16[512,1024]{1,0:T(8,128)(2,1)S(1)}) fusion(bf16[512,4096]{1,0:T(8,128)(2,1)} %param.17, s32[]{:T(128)S(6)} %select_n.174, s32[]{:T(128)S(6)} %select_n.173), kind=kLoop, calls=%fused_computation.49 | loop fusion | bytes 4194312 | tf_op jit(solution)/shard_map/dynamic_slice | solution.py:403
  83.9 0.1 constant_dynamic-slice_fusion.16
  84.1 0.8 constant_dynamic-slice_fusion.3
  84.9 1.1 collective-permute-start.3
  86.1 0.9 copy.30
  86.9 1.2 broadcast_add_fusion
  88.2 1.0 pad_maximum_fusion.5.refs_0_
  89.3 1.2 constant_dynamic-slice_fusion.4
  90.5 0.1 pad_maximum_fusion.refs_1_
  90.6 6.9 %softmax_stats.8 = f32[8,512]{1,0:T(8,128)S(1)} custom-call(bf16[512,256]{1,0:T(8,128)(2,1)S(1)} %pad_maximum_fusion.3.refs_0_, bf16[256,2048]{1,0:T(8,128)(2,1)S(1)} %pad_maximum_fusion.refs_1_, s32[512,1]{1,0:T(8,128)S(1)} %get-tuple-element.21.refs_2_), custom_call_target="tpu_custom_call" | custom-call | flops 512 | bytes 512 | tf_op jit(solution)/shard_map/softmax_stats/pallas_call | solution.py:368
  97.5 1.0 constant_dynamic-slice_fusion
  98.5 6.3 %softmax_stats.9 = f32[8,512]{1,0:T(8,128)S(1)} custom-call(bf16[512,64]{1,0:T(8,128)(2,1)S(1)} %pad_maximum_fusion.5.refs_0_, bf16[64,2048]{1,0:T(8,128)(2,1)S(1)} %pad_maximum_fusion.4.refs_1_, s32[512,1]{1,0:T(8,128)S(1)} %get-tuple-element.20.refs_2_), custom_call_target="tpu_custom_call" | custom-call | flops 512 | bytes 512 | tf_op jit(solution)/shard_map/softmax_stats/pallas_call | solution.py:368
  104.8 3.5 %softmax_stats.5.refs_5_ = f32[512,128]{1,0:T(8,128)S(1)} custom-call(bf16[512,512]{1,0:T(8,128)(2,1)S(1)} %get-tuple-element.17.refs_0_, bf16[512,512]{1,0:T(8,128)(2,1)S(1)} %get-tuple-element.16.refs_1_, bf16[512,512]{1,0:T(8,128)(2,1)S(1)} %copy-done.1, bf16[512,512]{1,0:T(8,128)(2,1)} %collective-permute-done.4.refs_3_, ...), custom_call_target="tpu_custom_call" | custom-call | flops 512 | bytes 512 | tf_op jit(solution)/shard_map/softmax_stats/pallas_call | solution.py:368
  108.3 18.2 %collective-permute-done.3.refs_3_ = bf16[512,1024]{1,0:T(8,128)(2,1)} collective-permute-done((bf16[512,1024]{1,0:T(8,128)(2,1)}, bf16[512,1024]{1,0:T(8,128)(2,1)}, u32[]{:S(2)}, u32[]{:S(2)}) %collective-permute-start.3) | collective-permute-done | bytes 1048608 | tf_op jit(solution)/shard_map/ppermute | solution.py:397
  126.6 6.0 %softmax_stats.6.refs_5_ = f32[512,128]{1,0:T(8,128)S(1)} custom-call(bf16[512,512]{1,0:T(8,128)(2,1)S(1)} %get-tuple-element.17.refs_0_, bf16[512,512]{1,0:T(8,128)(2,1)S(1)} %get-tuple-element.16.refs_1_, bf16[512,1024]{1,0:T(8,128)(2,1)S(1)} %get-tuple-element.15.refs_2_, bf16[512,1024]{1,0:T(8,128)(2,1)} %collective-permute-done.3.refs_3_, ...), custom_call_target="tpu_custom_call" | custom-call | flops 512 | bytes 512 | tf_op jit(solution)/shard_map/softmax_stats/pallas_call | solution.py:368
  132.6 3.6 %softmax_stats.7 = f32[8,512]{1,0:T(8,128)S(1)} custom-call(bf16[512,512]{1,0:T(8,128)(2,1)S(1)} %get-tuple-element.17.refs_0_, bf16[512,512]{1,0:T(8,128)(2,1)S(1)} %get-tuple-element.16.refs_1_, bf16[512,512]{1,0:T(8,128)(2,1)S(1)} %get-tuple-element.12.refs_2_, bf16[512,512]{1,0:T(8,128)(2,1)} %collective-permute-done.1.refs_3_, ...), custom_call_target="tpu_custom_call" | custom-call | flops 512 | bytes 512 | tf_op jit(solution)/shard_map/softmax_stats/pallas_call | solution.py:368
  136.3 6.1 %fusion.13 = (f32[256]{0:T(256)S(1)}, f32[256,2048]{1,0:T(8,128)S(1)}) fusion(bf16[256,2048]{1,0:T(8,128)(2,1)} %collective-permute-done.6, bf16[2048,2048]{1,0:T(8,128)(2,1)} %param.12, bf16[256,4096]{1,0:T(8,128)(2,1)S(1)} %copy-done.7, s32[]{:T(128)S(6)} %select_n.175), kind=kOutput, calls=%fused_computation.61 | convolution fusion | flops 2149056256 | bytes 12583940 | tf_op jit(solution)/shard_map/dot_general | solution.py:440
  142.4 0.6 exponential_reduce_fusion
  143.1 11.3 %totals.1 = f32[4,256]{1,0:T(4,128)S(1)} custom-call(f32[2,16,256]{2,1,0:T(8,128)S(1)} %bitcast.37, f32[4,256]{1,0:T(4,128)S(1)} %pad_maximum_fusion.6.head_ref, f32[3,256]{1,0:T(4,128)S(1)} %fusion.14.clus_ref, s32[1,256]{1,0:T(1,128)S(1)} %bitcast.39, f32[3,256]{1,0:T(4,128)S(1)} %convert_bitcast_fusion.flag_ref), custom_call_target="tpu_custom_call" | custom-call | tf_op jit(solution)/shard_map/totals/pallas_call | solution.py:313
  154.5 0.6 slice.46
  155.0 0.6 slice_bitcast_fusion
  (62 shorter events, 0.6 us)
Async XLA Ops:
  0.6 11.8 %copy-start = (bf16[256,1024]{1,0:T(8,128)(2,1)S(1)}, bf16[256,1024]{1,0:T(8,128)(2,1)}, u32[]{:S(2)}) copy-start(bf16[256,1024]{1,0:T(8,128)(2,1)} %param.14) | copy-start | bytes 1572868
  0.6 84.3 %collective-permute-start.2 = (s32[256]{0:T(256)}, s32[256]{0:T(256)S(1)}, u32[]{:S(2)}, u32[]{:S(2)}) collective-permute-start(s32[256]{0:T(256)} %param.20), channel_id=1, source_target_pairs={{0,1},{1,0},{2,3},{3,2},{4,5},{5,4},{6,7},{7,6},{8,9},{9,8},{10,11... | collective-permute-start | bytes 3080 | tf_op jit(solution)/shard_map/ppermute | solution.py:397
  4.6 6.1 %copy-start.6 = (bf16[256,4096]{1,0:T(8,128)(2,1)S(1)}, bf16[256,4096]{1,0:T(8,128)(2,1)}, u32[]{:S(2)}) copy-start(bf16[256,4096]{1,0:T(8,128)(2,1)} %param.11) | copy-start | bytes 6291460
  4.6 6.1 %copy-start.12 = (bf16[4096,3]{0,1:T(4,128)(2,1)S(1)}, bf16[4096,3]{0,1:T(4,128)(2,1)}, u32[]{:S(2)}) copy-start(bf16[4096,3]{0,1:T(4,128)(2,1)} %param.13) | copy-start | bytes 73732
  4.6 10.9 %collective-permute-start = (bf16[64,2048]{1,0:T(8,128)(2,1)}, bf16[64,2048]{1,0:T(8,128)(2,1)S(1)}, u32[]{:S(2)}, u32[]{:S(2)}) collective-permute-start(bf16[64,2048]{1,0:T(8,128)(2,1)} %dynamic_slice.64), channel_id=1, source_target_pairs={{0,1},{1,0},{2,3},{3,2},{4,5},{5,4},{6,7},{7,6},{8,9},{9,8},{10,11... | collective-permute-start | bytes 786440 | tf_op jit(solution)/shard_map/ppermute | solution.py:397
  8.6 2.8 %copy-start.15 = (s32[256,3]{0,1:T(4,128)S(1)}, s32[256,3]{0,1:T(4,128)}, u32[]{:S(2)}) copy-start(s32[256,3]{0,1:T(4,128)} %param.21) | copy-start | bytes 9220
  8.6 2.8 %copy-start.14 = (bf16[256,64]{0,1:T(8,128)(2,1)S(1)}, bf16[256,64]{0,1:T(8,128)(2,1)}, u32[]{:S(2)}) copy-start(bf16[256,64]{0,1:T(8,128)(2,1)} %param.16) | copy-start | bytes 98308
  8.6 3.6 %copy-start.11 = (bf16[256,256]{1,0:T(8,128)(2,1)S(1)}, bf16[256,256]{1,0:T(8,128)(2,1)}, u32[]{:S(2)}) copy-start(bf16[256,256]{1,0:T(8,128)(2,1)} %param.15) | copy-start | bytes 393220
  9.5 79.8 %collective-permute-start.5 = (bf16[160,2048]{1,0:T(8,128)(2,1)}, bf16[160,2048]{1,0:T(8,128)(2,1)}, u32[]{:S(2)}, u32[]{:S(2)}) collective-permute-start(bf16[160,2048]{1,0:T(8,128)(2,1)} %pad_maximum_fusion.2), channel_id=1, source_target_pairs={{0,1},{1,0},{2,3},{3,2},{4,5},{5,4},{6,7},{7,6},{8,9},{9,8},{10,11... | collective-permute-start | bytes 1966088 | tf_op jit(solution)/shard_map/ppermute | solution.py:397
  52.3 84.0 %collective-permute-start.6 = (bf16[256,2048]{1,0:T(8,128)(2,1)}, bf16[256,2048]{1,0:T(8,128)(2,1)}, u32[]{:S(2)}, u32[]{:S(2)}) collective-permute-start(bf16[256,2048]{1,0:T(8,128)(2,1)} %convolution_convert_fusion), channel_id=1, source_target_pairs={{0,1},{1,0},{2,3},{3,2},{4,5},{5,4},{6,7},{7,6},{8,9},{9,8},{10,11... | collective-permute-start | bytes 3145736 | tf_op jit(solution)/shard_map/ppermute | solution.py:397
  79.0 25.8 %collective-permute-start.4 = (bf16[512,512]{1,0:T(8,128)(2,1)}, bf16[512,512]{1,0:T(8,128)(2,1)}, u32[]{:S(2)}, u32[]{:S(2)}) collective-permute-start(bf16[512,512]{1,0:T(8,128)(2,1)} %get-tuple-element.10), channel_id=1, source_target_pairs={{0,1},{1,0},{2,3},{3,2},{4,5},{5,4},{6,7},{7,6},{8,9},{9,8},{10,11... | collective-permute-start | bytes 1572872 | tf_op jit(solution)/shard_map/ppermute | solution.py:397
  80.2 52.5 %collective-permute-start.1 = (bf16[512,512]{1,0:T(8,128)(2,1)}, bf16[512,512]{1,0:T(8,128)(2,1)}, u32[]{:S(2)}, u32[]{:S(2)}) collective-permute-start(bf16[512,512]{1,0:T(8,128)(2,1)} %get-tuple-element.11), channel_id=1, source_target_pairs={{0,1},{1,0},{2,3},{3,2},{4,5},{5,4},{6,7},{7,6},{8,9},{9,8},{10,11... | collective-permute-start | bytes 1572872 | tf_op jit(solution)/shard_map/ppermute | solution.py:397
  80.6 3.4 %copy-start.5 = (bf16[512,1024]{1,0:T(8,128)(2,1)S(1)}, bf16[512,1024]{1,0:T(8,128)(2,1)}, u32[]{:S(2)}) copy-start(bf16[512,1024]{1,0:T(8,128)(2,1)} %slice.49) | copy-start | bytes 3145732
  83.9 2.1 %copy-start.4 = (s32[256]{0:T(256)S(1)}, s32[256]{0:T(256)}, u32[]{:S(2)}) copy-start(s32[256]{0:T(256)} %param.20) | copy-start | bytes 3076
  84.9 3.3 %copy-start.9 = (bf16[512,32]{1,0:T(8,128)(2,1)S(1)}, bf16[512,32]{1,0:T(8,128)(2,1)}, u32[]{:S(2)}) copy-start(bf16[512,32]{1,0:T(8,128)(2,1)} %get-tuple-element.26) | copy-start | bytes 98308
  84.9 41.7 %collective-permute-start.3 = (bf16[512,1024]{1,0:T(8,128)(2,1)}, bf16[512,1024]{1,0:T(8,128)(2,1)}, u32[]{:S(2)}, u32[]{:S(2)}) collective-permute-start(bf16[512,1024]{1,0:T(8,128)(2,1)} %get-tuple-element.14), channel_id=1, source_target_pairs={{0,1},{1,0},{2,3},{3,2},{4,5},{5,4},{6,7},{7,6},{8,9},{9,8},{10,11... | collective-permute-start | bytes 3145736 | tf_op jit(solution)/shard_map/ppermute | solution.py:397
  86.9 3.5 %copy-start.8 = (bf16[128,2048]{1,0:T(8,128)(2,1)S(1)}, bf16[128,2048]{1,0:T(8,128)(2,1)}, u32[]{:S(2)}) copy-start(bf16[128,2048]{1,0:T(8,128)(2,1)} %get-tuple-element.18) | copy-start | bytes 1572868
  90.5 8.0 %copy-start.10 = (bf16[32,2048]{1,0:T(8,128)(2,1)S(1)}, bf16[32,2048]{1,0:T(8,128)(2,1)}, u32[]{:S(2)}) copy-start(bf16[32,2048]{1,0:T(8,128)(2,1)} %get-tuple-element.24) | copy-start | bytes 393220
  90.5 14.4 %copy-start.1 = (bf16[512,512]{1,0:T(8,128)(2,1)S(1)}, bf16[512,512]{1,0:T(8,128)(2,1)}, u32[]{:S(2)}) copy-start(bf16[512,512]{1,0:T(8,128)(2,1)} %get-tuple-element.13.refs_2_) | copy-start | bytes 1572868
  97.5 35.1 %copy-start.2 = (f32[8,512]{1,0:T(8,128)}, f32[8,512]{1,0:T(8,128)S(1)}, u32[]{:S(2)}) copy-start(f32[8,512]{1,0:T(8,128)S(1)} %softmax_stats.8) | copy-start | bytes 49156
  104.8 27.8 %copy-start.3 = (f32[8,512]{1,0:T(8,128)}, f32[8,512]{1,0:T(8,128)S(1)}, u32[]{:S(2)}) copy-start(f32[8,512]{1,0:T(8,128)S(1)} %softmax_stats.9) | copy-start | bytes 49156
  132.6 3.6 %copy-start.16 = (f32[16]{0:T(128)S(1)}, f32[16]{0:T(128)}, u32[]{:S(2)}) copy-start(f32[16]{0:T(128)} %pad.7.clone) | copy-start | bytes 196
  132.6 3.7 %copy-start.7 = (bf16[256,4096]{1,0:T(8,128)(2,1)S(1)}, bf16[256,4096]{1,0:T(8,128)(2,1)}, u32[]{:S(2)}) copy-start(bf16[256,4096]{1,0:T(8,128)(2,1)} %param.11) | copy-start | bytes 6291460
  132.6 3.6 %slice-start = ((f32[8,512]{1,0:T(8,128)}), f32[4,512]{1,0:T(4,128)S(1)}, s32[]{:S(2)}) async-start(f32[8,512]{1,0:T(8,128)} %copy-done.2), calls=%async_computation | async-start | bytes 16384 | tf_op jit(solution)/shard_map/slice | solution.py:471
  132.6 3.6 %slice-start.1 = ((f32[8,512]{1,0:T(8,128)}), f32[4,512]{1,0:T(4,128)S(1)}, s32[]{:S(2)}) async-start(f32[8,512]{1,0:T(8,128)} %copy-done.3), calls=%async_computation.1 | async-start | bytes 16384 | tf_op jit(solution)/shard_map/slice | solution.py:471
  136.3 6.1 %copy-start.13 = (s32[2048]{0:T(1024)S(1)}, s32[2048]{0:T(1024)}, u32[]{:S(2)}) copy-start(s32[2048]{0:T(1024)} %iota_add_fusion) | copy-start | bytes 24580
  142.4 0.6 copy-start.17
